TPU v7x, 32 devices: a whole 2x2x4 slice. The times are simulated.
32 devices in a mesh: seq: 8 (over y, x, core), head: 4 (over z).
Axes of the slice: x: 2, y: 2, z: 4, core: 2. Of those that a mesh axis runs over, the one named last changes fastest.
Arguments:
- queries: bfloat16 [1024, 6144], P('seq', 'head'), may hold values from -60 to 60
- keys: bfloat16 [1024, 6144], P('seq', 'head'), may hold values from -6 to 6
- values: bfloat16 [1024, 6144], P('seq', 'head'), may hold values from -6 to 6
- band: int32 [48], P('head'), may hold values from 16 to 64
- picks: int32 [8, 16], P('seq'), may hold values from 0 to 127, as said below
- w_out: bfloat16 [6144, 6144], P('seq', 'head'), may hold values from -0.078125 to 0.078125
Outputs:
- output: bfloat16 [1024, 6144], P(('seq', 'head'))
Inputs may be any that keep to these rules, and one draw needn't show every extreme that they name: The 16 entries of a row of picks are distinct.
All inputs are finite; a program needn't handle non-finite values.
Results may differ from a plain program's by a relative error of at most 0.015.
Values may be sent and summed in bfloat16 or wider, within the bound.
No kernel may reach another device: no remote copies, remote signals or barrier semaphores. Data moves between devices by JAX's collectives and lax.ppermute only.
A program may use at most 128 MiB of HBM per device.

v0:
```python
import functools
import math

import jax
import jax.numpy as jnp
from jax import lax
from jax.experimental import pallas as pl
from jax.experimental.pallas import tpu as pltpu
from jax.sharding import PartitionSpec as P

BLOCK = 128
HALO = 64
NEGATIVE_FILL = -1e30
LAST = (((1,), (1,)), ((), ()))
BF16 = jnp.bfloat16
BRIEF = pl.CostEstimate(flops=0, bytes_accessed=0, transcendentals=0)
LONGER = pl.CostEstimate(flops=1_100_000_000, bytes_accessed=3_000_000, transcendentals=0)
PARAMS = pltpu.CompilerParams(vmem_limit_bytes=32 << 20)


def vmem():
    return pl.BlockSpec(memory_space=pltpu.VMEM)


def smem():
    return pl.BlockSpec(memory_space=pltpu.SMEM)


def hbm():
    return pl.BlockSpec(memory_space=pltpu.HBM)


def shaped(*shape):
    return pltpu.VMEM(shape, BF16)


def far_away(*arrays):
    return [pltpu.with_memory_space_constraint(array, pltpu.HBM) for array in arrays]


def column_of(count, width, number):
    row = lax.broadcasted_iota(jnp.int32, (count, width), 0)
    found = jnp.zeros((count, width), jnp.int32)
    for r in range(count):
        found = jnp.where(row == r, number(r), found)
    return found


def pick_kernel(
    picks_ref, band_ref, q_hbm, k_hbm, v_hbm, summary_ref, halo_ref, width_ref, q_ref, k_ref, v_ref, sems
):
    per_block = picks_ref.shape[1]
    copies = [
        pltpu.make_async_copy(ref, into, sems.at[part])
        for part, (ref, into) in enumerate(((k_hbm, k_ref), (v_hbm, v_ref), (q_hbm, q_ref)))
    ]
    for copy in copies:
        copy.start()
    wanted = column_of(per_block, BLOCK, lambda r: picks_ref[0, r])
    width_ref[...] = column_of(*width_ref.shape, lambda r: band_ref[r])
    column = lax.broadcasted_iota(jnp.int32, (per_block, BLOCK), 1)
    chosen = jnp.where(column == wanted, 1.0, 0.0).astype(BF16)
    for part, ref in enumerate((k_ref, v_ref)):
        copies[part].wait()
        taken = jnp.dot(chosen, ref[...], preferred_element_type=jnp.float32)
        summary_ref[part] = taken.astype(BF16)
        halo_ref[part] = ref[BLOCK - HALO :, :]
    copies[2].wait()


def stack_kernel(*refs):
    for k, ref in enumerate(refs[:-1]):
        refs[-1][k] = ref[...]


def attend_kernel(low, width_ref, q_ref, k_ref, v_ref, *refs):
    halo_ref, mine_ref, other_ref = (refs if low else (None,) + refs)[:3]
    out_ref = refs[-1]
    size = BLOCK
    heads = q_ref.shape[1] // size
    start, count = (0, HALO) if low else (HALO, BLOCK - HALO)
    reach = start + count
    chips, unused, per_block, unused = mine_ref.shape
    far_rows = chips * per_block
    place = lax.axis_index("seq")
    chip = place // 2
    core = lax.rem(place, 2)
    scale = 1.0 / math.sqrt(size)
    never = 4 * BLOCK

    def distance(columns):
        row = lax.broadcasted_iota(jnp.int32, (count, columns), 0) + start
        return row - lax.broadcasted_iota(jnp.int32, (count, columns), 1)

    gap = distance(reach)
    gaps = [jnp.where(gap >= 0, gap, never)]
    if low:
        gaps.append(jnp.where(place > 0, distance(HALO) + HALO, never))
    far_chip = (lax.broadcasted_iota(jnp.int32, (count, far_rows), 1) // per_block) ^ chip
    gaps.append(jnp.where(far_chip * 2 + core < place, 0, never))
    gaps.append(jnp.where(far_chip * 2 + (1 - core) < place, 0, never))
    gap = jnp.concatenate(gaps, 1)
    listed = gap.shape[1]
    some = 2 if heads % 2 == 0 else 1
    starts = range(0, heads, some)

    def listing(part, own, first):
        cols = slice(first * size, (first + some) * size)
        return jnp.concatenate(
            [own[:reach, cols]]
            + ([halo_ref[part, :, cols]] if low else [])
            + [ref[:, part, :, cols].reshape(far_rows, some * size) for ref in (mine_ref, other_ref)],
            0,
        )

    scores = []
    for first in starts:
        query = q_ref[start:reach, first * size : (first + some) * size]
        if some == 2:
            zero = jnp.zeros((count, size), BF16)
            query = jnp.concatenate(
                [
                    jnp.concatenate([query[:, :size], zero], 1),
                    jnp.concatenate([zero, query[:, size:]], 1),
                ],
                0,
            )
        scores.append(
            lax.dot_general(query, listing(0, k_ref, first), LAST, preferred_element_type=jnp.float32)
        )
    weights, totals = [], []
    for h in range(heads):
        valid = gap < width_ref[h : h + 1, :listed]
        rows = slice(h % some * count, (h % some + 1) * count)
        part = jnp.where(valid, scores[h // some][rows] * scale, NEGATIVE_FILL)
        largest = jnp.max(part, axis=1, keepdims=True)
        part = jnp.where(valid, jnp.exp(part - largest), 0.0)
        totals.append(jnp.sum(part, axis=1, keepdims=True))
        weights.append(part.astype(BF16))
    for first in starts:
        rounded = jnp.concatenate(weights[first : first + some], 0)
        mixed = jnp.dot(rounded, listing(1, v_ref, first), preferred_element_type=jnp.float32)
        for j in range(some):
            taken = mixed[j * count : (j + 1) * count, j * size : (j + 1) * size]
            out_ref[:, (first + j) * size : (first + j + 1) * size] = (taken / totals[first + j]).astype(BF16)


def turn_kernel(mine_hbm, other_ref, order_ref, out_ref, mine_ref, sem):
    core = lax.rem(lax.axis_index("seq"), 2)
    wide = mine_ref.shape[0]
    step = math.gcd(wide, 128)
    copy = pltpu.make_async_copy(mine_hbm, mine_ref, sem)
    copy.start()
    for which, ref in ((1 - core, other_ref), (core, mine_ref)):
        if ref is mine_ref:
            copy.wait()
        for n in range(0, wide, step):
            out_ref[which, :, n : n + step] = ref[n : n + step, :].T


def project_kernel(high_ref, low_ref, turned_ref, *refs):
    send_ref, keep_ref = refs[-2:]
    side = lax.rem(lax.axis_index("head"), 2)
    rows_in = [ref[part] for part in (1 - side, side) for ref in (high_ref, low_ref)]
    rows_in = jnp.concatenate(rows_in, 0)
    for which in range(2):
        found = jnp.dot(rows_in, turned_ref[which], preferred_element_type=jnp.float32)
        found = found.astype(BF16).reshape((2,) + send_ref.shape[1:])
        send_ref[which] = found[0]
        keep_ref[which] = found[1]


def split_kernel(came_ref, keep_ref, *refs):
    away_ref, stay_ref = refs[-2:]
    side = lax.axis_index("head") // 2
    for ref, which in ((away_ref, side), (stay_ref, 1 - side)):
        total = came_ref[:, which].astype(jnp.float32) + keep_ref[:, which].astype(jnp.float32)
        ref[...] = total.astype(BF16)


def join_kernel(chunks, *refs):
    out_ref = refs[-1]
    wide = refs[0].shape[-1]
    chip = lax.axis_index("seq") // 2
    upper = lax.axis_index("head") // 2
    for n, (high, low) in enumerate(chunks):
        total = refs[2 * n][...].astype(jnp.float32) + refs[2 * n + 1][...].astype(jnp.float32)
        total = total.astype(BF16)
        source = chip ^ (high if high == low else jnp.where(upper == 1, high, low))
        if len(out_ref.shape) == 4:
            out_ref[source] = total
            continue
        for c in range(2):
            start = pl.multiple_of(source * (2 * wide), 128)
            out_ref[:, pl.ds(start + c * wide, wide)] = total[c]


def order_of_projection(n, keeps, stays, found):
    if n == 3:
        return [keeps[2], stays[1], found[0][0]]
    return [keeps[n - 1]] if 0 < n < 3 else []


def order_of_split(n, found):
    return [found[1][1]] if n in (2, 3) else []


def local(queries, keys, values, band, picks, w_out):
    heads = band.shape[0]
    tok_rows, feat = queries.shape
    per_block = picks.shape[1]
    seq = lax.axis_size("seq")
    groups = lax.axis_size("head")
    wide = w_out.shape[0]
    rows = tok_rows // groups
    chips = seq // 2
    half = groups // 2

    def swap(value, k, z):
        if k == 0:
            return lax.ppermute(value, "head", [(i, i ^ z) for i in range(groups)])
        if z == 0:
            return lax.ppermute(value, "seq", [(i, i ^ k) for i in range(seq)])
        pairs = [
            (s * groups + h, (s ^ k) * groups + (h ^ z)) for s in range(seq) for h in range(groups)
        ]
        return lax.ppermute(value, ("seq", "head"), pairs)

    other_w = swap(w_out, 1, 0)
    listed = BLOCK + seq * per_block
    summary, halo, width, queries, keys, values = pl.pallas_call(
        pick_kernel,
        out_shape=(
            shaped(2, per_block, feat),
            shaped(2, HALO, feat),
            pltpu.VMEM((heads, listed), jnp.int32),
        )
        + (shaped(tok_rows, feat),) * 3,
        in_specs=[smem(), smem(), hbm(), hbm(), hbm()],
        out_specs=(vmem(),) * 6,
        scratch_shapes=[pltpu.SemaphoreType.DMA((3,))],
        compiler_params=PARAMS,
    )(*far_away(picks, band, queries, keys, values))
    far = [summary] + [swap(summary, 2 * k, 0) for k in range(1, chips)]
    halo = lax.ppermute(halo, "seq", [(i, i + 1) for i in range(seq - 1)])
    mine = pl.pallas_call(
        stack_kernel,
        out_shape=shaped(chips, 2, per_block, feat),
        in_specs=[vmem()] * chips,
        out_specs=vmem(),
        compiler_params=PARAMS,
    )(*far)
    other = swap(mine, 1, 0)
    turned = pl.pallas_call(
        turn_kernel,
        out_shape=shaped(2, feat, wide),
        in_specs=[hbm(), vmem(), pl.BlockSpec(memory_space=pl.ANY)],
        out_specs=vmem(),
        scratch_shapes=[pltpu.VMEM((wide, feat), BF16), pltpu.SemaphoreType.DMA(())],
        compiler_params=PARAMS,
    )(*far_away(w_out), other_w, mine)

    def attended(low, behind, order=()):
        return pl.pallas_call(
            functools.partial(attend_kernel, low),
            out_shape=shaped(HALO if low else tok_rows - HALO, feat),
            in_specs=[vmem()] * (6 + len(behind)) + [pl.BlockSpec(memory_space=pl.ANY)] * len(order),
            out_specs=vmem(),
            compiler_params=PARAMS,
            cost_estimate=LONGER,
        )(width, queries, keys, values, *behind, mine, other, *order).reshape(half, rows, feat)

    highs = [attended(False, (), (halo, turned))]
    lows = [attended(True, (halo,), (turned,))]
    for k in range(1, chips):
        if k == 3:
            highs.append(swap(highs[1], 4, 0))
            lows.append(swap(lows[2], 2, 0))
            continue
        highs.append(swap(highs[0], 2 * k, 0))
        lows.append(swap(lows[0], 2 * k, 0))
    chunks = [(0, 0)] + [(1, 2), (2, 1)][: 2 if chips > 2 else 0] + ([(1, 1)] if chips == 2 else [])
    chunks += [(k, k) for k in range(3, chips)]

    def after(*arrays):
        return [pl.BlockSpec(memory_space=pl.ANY)] * len(arrays), arrays

    def projected(high, low, order):
        specs, arrays = after(*order)
        return pl.pallas_call(
            project_kernel,
            out_shape=(shaped(2, half, rows, wide),) * 2,
            in_specs=[vmem()] * 3 + specs,
            out_specs=(vmem(),) * 2,
            compiler_params=PARAMS,
            cost_estimate=BRIEF,
        )(highs[high], lows[low], turned, *arrays)

    def owned(value, high, low, leaves):
        if not leaves and high == low == 0:
            return value
        pairs = []
        for s in range(seq):
            for h in range(groups):
                k = low if (h >= half) == leaves else high
                pairs.append((s * groups + h, (s ^ 2 * k) * groups + (h ^ 2 * leaves)))
        return lax.ppermute(value, ("seq", "head"), pairs)

    sends, keeps, aways, stays, found = {}, {}, {}, {}, {}
    for n, (high, low) in enumerate(chunks):
        sends[n], keeps[n] = projected(high, low, order_of_projection(n, keeps, stays, found))
        came = swap(sends[n], 0, 1)
        specs, arrays = after(*order_of_split(n, found))
        aways[n], stays[n] = pl.pallas_call(
            split_kernel,
            out_shape=(shaped(2, rows, wide),) * 2,
            in_specs=[vmem()] * 2 + specs,
            out_specs=(vmem(),) * 2,
            compiler_params=PARAMS,
        )(came, keeps[n], *arrays)
        found[n] = (owned(aways[n], high, low, True), owned(stays[n], high, low, False))
    flat = wide % 128 == 0
    joined = pl.pallas_call(
        functools.partial(join_kernel, chunks),
        out_shape=jax.ShapeDtypeStruct((rows, seq * wide) if flat else (chips, 2, rows, wide), BF16),
        in_specs=[vmem()] * (2 * chips),
        out_specs=vmem(),
        compiler_params=PARAMS,
    )(*[piece for n in range(chips) for piece in found[n]])
    return joined if flat else joined.transpose(2, 0, 1, 3).reshape(rows, seq * wide)


def solution(mesh):
    placed = (
        P("seq", "head"),
        P("seq", "head"),
        P("seq", "head"),
        P("head"),
        P("seq", None),
        P("seq", "head"),
    )
    return jax.shard_map(
        local, mesh=mesh, in_specs=placed, out_specs=P(("seq", "head"), None), check_vma=False
    )
```

profile of v0, /device:TPU:0, one launch (start us, length us, event | category | flops | bytes accessed | tf_op | source)
XLA Modules:
  0.0 58.8 jit_solution(17827630941855235042)
XLA Ops:
  0.0 0.5 collective-permute-start.5
  0.5 2.1 %shard_map.64 = (bf16[2,16,1536]{2,1,0:T(8,128)(2,1)S(1)}, bf16[2,64,1536]{2,1,0:T(8,128)(2,1)S(1)}, s32[12,256]{1,0:T(8,128)S(1)}, bf16[128,1536]{1,0:T(8,128)(...) custom-call(s32[1,16]{1,0:T(1,128)} %picks_ref.1, s32[12]{0:T(128)} %band_ref.1, ...), custom_call_target="tpu_custom_call" | custom-call | tf_op jit(solution)/shard_map/pallas_call | solution.py:231
  2.5 2.6 %collective-permute-start = (bf16[2,16,1536]{2,1,0:T(8,128)(2,1)S(1)}, bf16[2,16,1536]{2,1,0:T(8,128)(2,1)S(1)}, u32[]{:S(2)}, u32[]{:S(2)}) collective-permute-start(bf16[2,16,1536]{2,1,0:T(8,128)(2,1)S(1)} %get-tuple-element.31.refs_0_), channel_id=1, source_target_pairs={{0,8},{4,12},{8,0},{12,4},{16,24},{20,28},{24,16},{28,20},{1,9},{5... | collective-permute-start | bytes 294920 | tf_op jit(solution)/shard_map/ppermute | solution.py:223
  5.1 1.5 %collective-permute-start.1 = (bf16[2,16,1536]{2,1,0:T(8,128)(2,1)S(1)}, bf16[2,16,1536]{2,1,0:T(8,128)(2,1)S(1)}, u32[]{:S(2)}, u32[]{:S(2)}) collective-permute-start(bf16[2,16,1536]{2,1,0:T(8,128)(2,1)S(1)} %get-tuple-element.31.refs_0_), channel_id=1, source_target_pairs={{0,16},{4,20},{8,24},{12,28},{16,0},{20,4},{24,8},{28,12},{1,17},{... | collective-permute-start | bytes 294920 | tf_op jit(solution)/shard_map/ppermute | solution.py:223
  6.6 0.0 collective-permute-start.2
  6.6 1.9 %collective-permute-start.4 = (bf16[2,64,1536]{2,1,0:T(8,128)(2,1)S(1)}, bf16[2,64,1536]{2,1,0:T(8,128)(2,1)S(1)}, u32[]{:S(2)}, u32[]{:S(2)}) collective-permute-start(bf16[2,64,1536]{2,1,0:T(8,128)(2,1)S(1)} %get-tuple-element.32), channel_id=1, source_target_pairs={{0,4},{4,8},{8,12},{12,16},{16,20},{20,24},{24,28},{1,5},{5,9},{9,... | collective-permute-start | bytes 1179656 | tf_op jit(solution)/shard_map/ppermute | solution.py:245
  8.5 0.1 collective-permute-done.refs_1_
  8.5 2.6 %collective-permute-done.1.refs_2_ = bf16[2,16,1536]{2,1,0:T(8,128)(2,1)S(1)} collective-permute-done((bf16[2,16,1536]{2,1,0:T(8,128)(2,1)S(1)}, bf16[2,16,1536]{2,1,0:T(8,128)(2,1)S(1)}, u32[]{:S(2)}, u32[]{:S(2)}) %collective-permute-start.1) | collective-permute-done | bytes 98336 | tf_op jit(solution)/shard_map/ppermute | solution.py:223
  11.1 1.0 %collective-permute-done.2.refs_3_ = bf16[2,16,1536]{2,1,0:T(8,128)(2,1)S(1)} collective-permute-done((bf16[2,16,1536]{2,1,0:T(8,128)(2,1)S(1)}, bf16[2,16,1536]{2,1,0:T(8,128)(2,1)S(1)}, u32[]{:S(2)}, u32[]{:S(2)}) %collective-permute-start.2) | collective-permute-done | bytes 98336 | tf_op jit(solution)/shard_map/ppermute | solution.py:223
  12.2 0.1 collective-permute-start.3
  12.2 0.0 collective-permute-done.5.other_ref
  12.3 2.3 %shard_map.66.refs_3_.turned_ref = bf16[2,1536,768]{2,1,0:T(8,128)(2,1)S(1)} custom-call(bf16[768,1536]{1,0:T(8,128)(2,1)} %mine_hbm.1, bf16[768,1536]{1,0:T(8,128)(2,1)S(1)} %collective-permute-done.5.other_ref, bf16[4,2,16,1536]{3,2,1,0:T(8,128)(2,1)S(1)} %shard_map.65.order_ref.refs_0_.refs_1_), custom_call_target="tpu_custom_call" | custom-call | tf_op jit(solution)/shard_map/pallas_call | solution.py:254
  14.6 0.0 collective-permute-done.3.refs_1_.refs_2_
  14.6 0.7 %shard_map.68 = bf16[64,1536]{1,0:T(8,128)(2,1)S(1)} custom-call(s32[12,256]{1,0:T(8,128)S(1)} %get-tuple-element.27.width_ref, bf16[128,1536]{1,0:T(8,128)(2,1)S(1)} %get-tuple-element.28.q_ref, bf16[128,1536]{1,0:T(8,128)(2,1)S(1)} %get-tuple-element.29.k_ref, bf16[128,1536]{1,0:T(8,128)(2,1)S(1)} %get-tuple-element.30.v_ref, ...), custom_call_target="tpu_custom_call" | custom-call | flops 1100000000 | bytes 3000000 | tf_op jit(solution)/shard_map/pallas_call | solution.py:264
  15.3 4.0 %collective-permute-start.9 = (bf16[2,32,1536]{2,1,0:T(8,128)(2,1)S(1)}, bf16[2,32,1536]{2,1,0:T(8,128)(2,1)S(1)}, u32[]{:S(2)}, u32[]{:S(2)}) collective-permute-start(bf16[2,32,1536]{2,1,0:T(8,128)(2,1)S(1)} %bitcast.5), channel_id=1, source_target_pairs={{0,16},{4,20},{8,24},{12,28},{16,0},{20,4},{24,8},{28,12},{1,17},{... | collective-permute-start | bytes 589832 | tf_op jit(solution)/shard_map/ppermute | solution.py:223
  19.3 0.7 %shard_map.67 = bf16[64,1536]{1,0:T(8,128)(2,1)S(1)} custom-call(s32[12,256]{1,0:T(8,128)S(1)} %get-tuple-element.27.width_ref, bf16[128,1536]{1,0:T(8,128)(2,1)S(1)} %get-tuple-element.28.q_ref, bf16[128,1536]{1,0:T(8,128)(2,1)S(1)} %get-tuple-element.29.k_ref, bf16[128,1536]{1,0:T(8,128)(2,1)S(1)} %get-tuple-element.30.v_ref, ...), custom_call_target="tpu_custom_call" | custom-call | flops 1100000000 | bytes 3000000 | tf_op jit(solution)/shard_map/pallas_call | solution.py:264
  20.0 0.7 %collective-permute-start.8 = (bf16[2,32,1536]{2,1,0:T(8,128)(2,1)S(1)}, bf16[2,32,1536]{2,1,0:T(8,128)(2,1)S(1)}, u32[]{:S(2)}, u32[]{:S(2)}) collective-permute-start(bf16[2,32,1536]{2,1,0:T(8,128)(2,1)S(1)} %bitcast.2), channel_id=1, source_target_pairs={{0,8},{4,12},{8,0},{12,4},{16,24},{20,28},{24,16},{28,20},{1,9},{5... | collective-permute-start | bytes 589832 | tf_op jit(solution)/shard_map/ppermute | solution.py:223
  20.6 0.8 %shard_map.69 = (bf16[2,2,32,768]{3,2,1,0:T(8,128)(2,1)S(1)}, bf16[2,2,32,768]{3,2,1,0:T(8,128)(2,1)S(1)}) custom-call(bf16[2,32,1536]{2,1,0:T(8,128)(2,1)S(1)} %bitcast.3, bf16[2,32,1536]{2,1,0:T(8,128)(2,1)S(1)} %bitcast.6, bf16[2,1536,768]{2,1,0:T(8,128)(2,1)S(1)} %shard_map.66.refs_3_.turned_ref), custom_call_target="tpu_custom_call" | custom-call | tf_op jit(solution)/shard_map/pallas_call | solution.py:290
  21.4 1.6 %collective-permute-start.6 = (bf16[2,2,32,768]{3,2,1,0:T(8,128)(2,1)S(1)}, bf16[2,2,32,768]{3,2,1,0:T(8,128)(2,1)S(1)}, u32[]{:S(2)}, u32[]{:S(2)}) collective-permute-start(bf16[2,2,32,768]{3,2,1,0:T(8,128)(2,1)S(1)} %get-tuple-element.33), channel_id=1, source_target_pairs={{0,1},{1,0},{2,3},{3,2},{4,5},{5,4},{6,7},{7,6},{8,9},{9,8},{10,11... | collective-permute-start | bytes 589832 | tf_op jit(solution)/shard_map/ppermute | solution.py:221
  23.1 1.4 %collective-permute-start.14 = (bf16[2,32,1536]{2,1,0:T(8,128)(2,1)S(1)}, bf16[2,32,1536]{2,1,0:T(8,128)(2,1)S(1)}, u32[]{:S(2)}, u32[]{:S(2)}) collective-permute-start(bf16[2,32,1536]{2,1,0:T(8,128)(2,1)S(1)} %bitcast.7), channel_id=1, source_target_pairs={{0,8},{4,12},{8,0},{12,4},{16,24},{20,28},{24,16},{28,20},{1,9},{5... | collective-permute-start | bytes 589832 | tf_op jit(solution)/shard_map/ppermute | solution.py:223
  24.5 0.0 collective-permute-start.13
  24.5 0.0 collective-permute-done.9.low_ref
  24.5 2.5 %collective-permute-done.8.high_ref = bf16[2,32,1536]{2,1,0:T(8,128)(2,1)S(1)} collective-permute-done((bf16[2,32,1536]{2,1,0:T(8,128)(2,1)S(1)}, bf16[2,32,1536]{2,1,0:T(8,128)(2,1)S(1)}, u32[]{:S(2)}, u32[]{:S(2)}) %collective-permute-start.8) | collective-permute-done | bytes 196640 | tf_op jit(solution)/shard_map/ppermute | solution.py:223
  27.0 0.8 %shard_map.71 = (bf16[2,2,32,768]{3,2,1,0:T(8,128)(2,1)S(1)}, bf16[2,2,32,768]{3,2,1,0:T(8,128)(2,1)S(1)}) custom-call(bf16[2,32,1536]{2,1,0:T(8,128)(2,1)S(1)} %collective-permute-done.8.high_ref, bf16[2,32,1536]{2,1,0:T(8,128)(2,1)S(1)} %collective-permute-done.9.low_ref, bf16[2,1536,768]{2,1,0:T(8,128)(2,1)S(1)} %shard_map.66.refs_3_.turned_ref, ...), custom_call_target="tpu_custom_call" | custom-call | tf_op jit(solution)/shard_map/pallas_call | solution.py:290
  27.8 1.9 %collective-permute-start.10 = (bf16[2,2,32,768]{3,2,1,0:T(8,128)(2,1)S(1)}, bf16[2,2,32,768]{3,2,1,0:T(8,128)(2,1)S(1)}, u32[]{:S(2)}, u32[]{:S(2)}) collective-permute-start(bf16[2,2,32,768]{3,2,1,0:T(8,128)(2,1)S(1)} %get-tuple-element.37), channel_id=1, source_target_pairs={{0,1},{1,0},{2,3},{3,2},{4,5},{5,4},{6,7},{7,6},{8,9},{9,8},{10,11... | collective-permute-start | bytes 589832 | tf_op jit(solution)/shard_map/ppermute | solution.py:221
  29.7 0.8 %collective-permute-start.19 = (bf16[2,32,1536]{2,1,0:T(8,128)(2,1)S(1)}, bf16[2,32,1536]{2,1,0:T(8,128)(2,1)S(1)}, u32[]{:S(2)}, u32[]{:S(2)}) collective-permute-start(bf16[2,32,1536]{2,1,0:T(8,128)(2,1)S(1)} %collective-permute-done.9.low_ref), channel_id=1, source_target_pairs={{0,8},{4,12},{8,0},{12,4},{16,24},{20,28},{24,16},{28,20},{1,9},{5... | collective-permute-start | bytes 589832 | tf_op jit(solution)/shard_map/ppermute | solution.py:223
  30.5 0.9 %collective-permute-start.18 = (bf16[2,32,1536]{2,1,0:T(8,128)(2,1)S(1)}, bf16[2,32,1536]{2,1,0:T(8,128)(2,1)S(1)}, u32[]{:S(2)}, u32[]{:S(2)}) collective-permute-start(bf16[2,32,1536]{2,1,0:T(8,128)(2,1)S(1)} %collective-permute-done.8.high_ref), channel_id=1, source_target_pairs={{0,16},{4,20},{8,24},{12,28},{16,0},{20,4},{24,8},{28,12},{1,17},{... | collective-permute-start | bytes 589832 | tf_op jit(solution)/shard_map/ppermute | solution.py:223
  31.5 0.0 collective-permute-done.14.low_ref
  31.5 2.6 %collective-permute-start.7 = (bf16[2,32,768]{2,1,0:T(8,128)(2,1)S(1)}, bf16[2,32,768]{2,1,0:T(8,128)(2,1)S(1)}, u32[]{:S(2)}, u32[]{:S(2)}) collective-permute-start(bf16[2,32,768]{2,1,0:T(8,128)(2,1)S(1)} %get-tuple-element.35), channel_id=1, source_target_pairs={{0,2},{1,3},{2,0},{3,1},{4,6},{5,7},{6,4},{7,5},{8,10},{9,11},{10,... | collective-permute-start | bytes 294920 | tf_op jit(solution)/shard_map/ppermute | solution.py:307
  34.1 0.8 %shard_map.73 = (bf16[2,2,32,768]{3,2,1,0:T(8,128)(2,1)S(1)}, bf16[2,2,32,768]{3,2,1,0:T(8,128)(2,1)S(1)}) custom-call(bf16[2,32,1536]{2,1,0:T(8,128)(2,1)S(1)} %collective-permute-done.13.high_ref, bf16[2,32,1536]{2,1,0:T(8,128)(2,1)S(1)} %collective-permute-done.14.low_ref, bf16[2,1536,768]{2,1,0:T(8,128)(2,1)S(1)} %shard_map.66.refs_3_.turned_ref, ...), custom_call_target="tpu_custom_call" | custom-call | tf_op jit(solution)/shard_map/pallas_call | solution.py:290
  34.9 1.2 %collective-permute-start.15 = (bf16[2,2,32,768]{3,2,1,0:T(8,128)(2,1)S(1)}, bf16[2,2,32,768]{3,2,1,0:T(8,128)(2,1)S(1)}, u32[]{:S(2)}, u32[]{:S(2)}) collective-permute-start(bf16[2,2,32,768]{3,2,1,0:T(8,128)(2,1)S(1)} %get-tuple-element.41), channel_id=1, source_target_pairs={{0,1},{1,0},{2,3},{3,2},{4,5},{5,4},{6,7},{7,6},{8,9},{9,8},{10,11... | collective-permute-start | bytes 589832 | tf_op jit(solution)/shard_map/ppermute | solution.py:221
  36.1 0.0 collective-permute-done.10.came_ref
  36.2 1.7 %collective-permute-done.7.refs_2_.refs_0_ = bf16[2,32,768]{2,1,0:T(8,128)(2,1)S(1)} collective-permute-done((bf16[2,32,768]{2,1,0:T(8,128)(2,1)S(1)}, bf16[2,32,768]{2,1,0:T(8,128)(2,1)S(1)}, u32[]{:S(2)}, u32[]{:S(2)}) %collective-permute-start.7) | collective-permute-done | bytes 98336 | tf_op jit(solution)/shard_map/ppermute | solution.py:307
  37.9 0.0 collective-permute-done.19.low_ref
  37.9 0.0 collective-permute-done.18.high_ref
  37.9 0.8 %shard_map.75 = (bf16[2,2,32,768]{3,2,1,0:T(8,128)(2,1)S(1)}, bf16[2,2,32,768]{3,2,1,0:T(8,128)(2,1)S(1)}) custom-call(bf16[2,32,1536]{2,1,0:T(8,128)(2,1)S(1)} %collective-permute-done.18.high_ref, bf16[2,32,1536]{2,1,0:T(8,128)(2,1)S(1)} %collective-permute-done.19.low_ref, bf16[2,1536,768]{2,1,0:T(8,128)(2,1)S(1)} %shard_map.66.refs_3_.turned_ref, ...), custom_call_target="tpu_custom_call" | custom-call | tf_op jit(solution)/shard_map/pallas_call | solution.py:290
  38.7 1.0 %collective-permute-start.20 = (bf16[2,2,32,768]{3,2,1,0:T(8,128)(2,1)S(1)}, bf16[2,2,32,768]{3,2,1,0:T(8,128)(2,1)S(1)}, u32[]{:S(2)}, u32[]{:S(2)}) collective-permute-start(bf16[2,2,32,768]{3,2,1,0:T(8,128)(2,1)S(1)} %get-tuple-element.45), channel_id=1, source_target_pairs={{0,1},{1,0},{2,3},{3,2},{4,5},{5,4},{6,7},{7,6},{8,9},{9,8},{10,11... | collective-permute-start | bytes 589832 | tf_op jit(solution)/shard_map/ppermute | solution.py:221
  39.7 0.9 %collective-permute-start.12 = (bf16[2,32,768]{2,1,0:T(8,128)(2,1)S(1)}, bf16[2,32,768]{2,1,0:T(8,128)(2,1)S(1)}, u32[]{:S(2)}, u32[]{:S(2)}) collective-permute-start(bf16[2,32,768]{2,1,0:T(8,128)(2,1)S(1)} %get-tuple-element.40.refs_1_), channel_id=1, source_target_pairs={{0,16},{1,17},{2,10},{3,11},{4,20},{5,21},{6,14},{7,15},{8,24},{9,... | collective-permute-start | bytes 294920 | tf_op jit(solution)/shard_map/ppermute | solution.py:307
  40.6 3.2 %collective-permute-start.11 = (bf16[2,32,768]{2,1,0:T(8,128)(2,1)S(1)}, bf16[2,32,768]{2,1,0:T(8,128)(2,1)S(1)}, u32[]{:S(2)}, u32[]{:S(2)}) collective-permute-start(bf16[2,32,768]{2,1,0:T(8,128)(2,1)S(1)} %get-tuple-element.39), channel_id=1, source_target_pairs={{0,10},{1,11},{2,16},{3,17},{4,14},{5,15},{6,20},{7,21},{8,2},{9,3... | collective-permute-start | bytes 294920 | tf_op jit(solution)/shard_map/ppermute | solution.py:307
  43.8 0.5 collective-permute-done.12.refs_0_.refs_3_
  44.4 3.0 %collective-permute-start.16 = (bf16[2,32,768]{2,1,0:T(8,128)(2,1)S(1)}, bf16[2,32,768]{2,1,0:T(8,128)(2,1)S(1)}, u32[]{:S(2)}, u32[]{:S(2)}) collective-permute-start(bf16[2,32,768]{2,1,0:T(8,128)(2,1)S(1)} %get-tuple-element.43), channel_id=1, source_target_pairs={{0,18},{1,19},{2,8},{3,9},{4,22},{5,23},{6,12},{7,13},{8,26},{9,27... | collective-permute-start | bytes 294920 | tf_op jit(solution)/shard_map/ppermute | solution.py:307
  47.4 2.0 %collective-permute-start.17 = (bf16[2,32,768]{2,1,0:T(8,128)(2,1)S(1)}, bf16[2,32,768]{2,1,0:T(8,128)(2,1)S(1)}, u32[]{:S(2)}, u32[]{:S(2)}) collective-permute-start(bf16[2,32,768]{2,1,0:T(8,128)(2,1)S(1)} %get-tuple-element.44), channel_id=1, source_target_pairs={{0,8},{1,9},{2,18},{3,19},{4,12},{5,13},{6,22},{7,23},{8,0},{9,1},... | collective-permute-start | bytes 294920 | tf_op jit(solution)/shard_map/ppermute | solution.py:307
  49.5 0.3 collective-permute-start.21
  49.8 1.9 %collective-permute-start.22 = (bf16[2,32,768]{2,1,0:T(8,128)(2,1)S(1)}, bf16[2,32,768]{2,1,0:T(8,128)(2,1)S(1)}, u32[]{:S(2)}, u32[]{:S(2)}) collective-permute-start(bf16[2,32,768]{2,1,0:T(8,128)(2,1)S(1)} %get-tuple-element.48), channel_id=1, source_target_pairs={{0,24},{1,25},{2,26},{3,27},{4,28},{5,29},{6,30},{7,31},{8,16},{9,... | collective-permute-start | bytes 294920 | tf_op jit(solution)/shard_map/ppermute | solution.py:307
  51.7 1.1 %collective-permute-done.16.refs_4_ = bf16[2,32,768]{2,1,0:T(8,128)(2,1)S(1)} collective-permute-done((bf16[2,32,768]{2,1,0:T(8,128)(2,1)S(1)}, bf16[2,32,768]{2,1,0:T(8,128)(2,1)S(1)}, u32[]{:S(2)}, u32[]{:S(2)}) %collective-permute-start.16) | collective-permute-done | bytes 98336 | tf_op jit(solution)/shard_map/ppermute | solution.py:307
  52.8 0.0 collective-permute-done.17.refs_5_
  52.9 5.1 %collective-permute-done.21.refs_6_ = bf16[2,32,768]{2,1,0:T(8,128)(2,1)S(1)} collective-permute-done((bf16[2,32,768]{2,1,0:T(8,128)(2,1)S(1)}, bf16[2,32,768]{2,1,0:T(8,128)(2,1)S(1)}, u32[]{:S(2)}, u32[]{:S(2)}) %collective-permute-start.21) | collective-permute-done | bytes 98336 | tf_op jit(solution)/shard_map/ppermute | solution.py:307
  57.9 0.8 %shard_map.77 = bf16[32,6144]{1,0:T(8,128)(2,1)} custom-call(bf16[2,32,768]{2,1,0:T(8,128)(2,1)S(1)} %collective-permute-done.7.refs_2_.refs_0_, bf16[2,32,768]{2,1,0:T(8,128)(2,1)S(1)} %get-tuple-element.36.refs_1_, bf16[2,32,768]{2,1,0:T(8,128)(2,1)S(1)} %collective-permute-done.11.refs_2_, ...), custom_call_target="tpu_custom_call" | custom-call | tf_op jit(solution)/shard_map/pallas_call | solution.py:323
  (12 shorter events, 0.2 us)
Async XLA Ops:
  0.0 12.2 %collective-permute-start.5 = (bf16[768,1536]{1,0:T(8,128)(2,1)}, bf16[768,1536]{1,0:T(8,128)(2,1)S(1)}, u32[]{:S(2)}, u32[]{:S(2)}) collective-permute-start(bf16[768,1536]{1,0:T(8,128)(2,1)} %mine_hbm.1), channel_id=1, source_target_pairs={{0,4},{4,0},{8,12},{12,8},{16,20},{20,16},{24,28},{28,24},{1,5},{5... | collective-permute-start | bytes 7077896 | tf_op jit(solution)/shard_map/ppermute | solution.py:223
  2.5 6.0 %collective-permute-start = (bf16[2,16,1536]{2,1,0:T(8,128)(2,1)S(1)}, bf16[2,16,1536]{2,1,0:T(8,128)(2,1)S(1)}, u32[]{:S(2)}, u32[]{:S(2)}) collective-permute-start(bf16[2,16,1536]{2,1,0:T(8,128)(2,1)S(1)} %get-tuple-element.31.refs_0_), channel_id=1, source_target_pairs={{0,8},{4,12},{8,0},{12,4},{16,24},{20,28},{24,16},{28,20},{1,9},{5... | collective-permute-start | bytes 294920 | tf_op jit(solution)/shard_map/ppermute | solution.py:223
  5.1 6.1 %collective-permute-start.1 = (bf16[2,16,1536]{2,1,0:T(8,128)(2,1)S(1)}, bf16[2,16,1536]{2,1,0:T(8,128)(2,1)S(1)}, u32[]{:S(2)}, u32[]{:S(2)}) collective-permute-start(bf16[2,16,1536]{2,1,0:T(8,128)(2,1)S(1)} %get-tuple-element.31.refs_0_), channel_id=1, source_target_pairs={{0,16},{4,20},{8,24},{12,28},{16,0},{20,4},{24,8},{28,12},{1,17},{... | collective-permute-start | bytes 294920 | tf_op jit(solution)/shard_map/ppermute | solution.py:223
  6.6 5.5 %collective-permute-start.2 = (bf16[2,16,1536]{2,1,0:T(8,128)(2,1)S(1)}, bf16[2,16,1536]{2,1,0:T(8,128)(2,1)S(1)}, u32[]{:S(2)}, u32[]{:S(2)}) collective-permute-start(bf16[2,16,1536]{2,1,0:T(8,128)(2,1)S(1)} %get-tuple-element.31.refs_0_), channel_id=1, source_target_pairs={{0,24},{4,28},{8,16},{12,20},{16,8},{20,12},{24,0},{28,4},{1,25},{... | collective-permute-start | bytes 294920 | tf_op jit(solution)/shard_map/ppermute | solution.py:223
  6.6 8.0 %collective-permute-start.4 = (bf16[2,64,1536]{2,1,0:T(8,128)(2,1)S(1)}, bf16[2,64,1536]{2,1,0:T(8,128)(2,1)S(1)}, u32[]{:S(2)}, u32[]{:S(2)}) collective-permute-start(bf16[2,64,1536]{2,1,0:T(8,128)(2,1)S(1)} %get-tuple-element.32), channel_id=1, source_target_pairs={{0,4},{4,8},{8,12},{12,16},{16,20},{20,24},{24,28},{1,5},{5,9},{9,... | collective-permute-start | bytes 1179656 | tf_op jit(solution)/shard_map/ppermute | solution.py:245
  12.2 2.5 %collective-permute-start.3 = (bf16[4,2,16,1536]{3,2,1,0:T(8,128)(2,1)S(1)}, bf16[4,2,16,1536]{3,2,1,0:T(8,128)(2,1)S(1)}, u32[]{:S(2)}, u32[]{:S(2)}) collective-permute-start(bf16[4,2,16,1536]{3,2,1,0:T(8,128)(2,1)S(1)} %shard_map.65.order_ref.refs_0_.refs_1_), channel_id=1, source_target_pairs={{0,4},{4,0},{8,12},{12,8},{16,20},{20,16},{24,28},{28,24},{1,5},{5... | collective-permute-start | bytes 1179656 | tf_op jit(solution)/shard_map/ppermute | solution.py:223
  15.3 9.2 %collective-permute-start.9 = (bf16[2,32,1536]{2,1,0:T(8,128)(2,1)S(1)}, bf16[2,32,1536]{2,1,0:T(8,128)(2,1)S(1)}, u32[]{:S(2)}, u32[]{:S(2)}) collective-permute-start(bf16[2,32,1536]{2,1,0:T(8,128)(2,1)S(1)} %bitcast.5), channel_id=1, source_target_pairs={{0,16},{4,20},{8,24},{12,28},{16,0},{20,4},{24,8},{28,12},{1,17},{... | collective-permute-start | bytes 589832 | tf_op jit(solution)/shard_map/ppermute | solution.py:223
  20.0 7.0 %collective-permute-start.8 = (bf16[2,32,1536]{2,1,0:T(8,128)(2,1)S(1)}, bf16[2,32,1536]{2,1,0:T(8,128)(2,1)S(1)}, u32[]{:S(2)}, u32[]{:S(2)}) collective-permute-start(bf16[2,32,1536]{2,1,0:T(8,128)(2,1)S(1)} %bitcast.2), channel_id=1, source_target_pairs={{0,8},{4,12},{8,0},{12,4},{16,24},{20,28},{24,16},{28,20},{1,9},{5... | collective-permute-start | bytes 589832 | tf_op jit(solution)/shard_map/ppermute | solution.py:223
  21.4 9.1 %collective-permute-start.6 = (bf16[2,2,32,768]{3,2,1,0:T(8,128)(2,1)S(1)}, bf16[2,2,32,768]{3,2,1,0:T(8,128)(2,1)S(1)}, u32[]{:S(2)}, u32[]{:S(2)}) collective-permute-start(bf16[2,2,32,768]{3,2,1,0:T(8,128)(2,1)S(1)} %get-tuple-element.33), channel_id=1, source_target_pairs={{0,1},{1,0},{2,3},{3,2},{4,5},{5,4},{6,7},{7,6},{8,9},{9,8},{10,11... | collective-permute-start | bytes 589832 | tf_op jit(solution)/shard_map/ppermute | solution.py:221
  23.1 8.4 %collective-permute-start.14 = (bf16[2,32,1536]{2,1,0:T(8,128)(2,1)S(1)}, bf16[2,32,1536]{2,1,0:T(8,128)(2,1)S(1)}, u32[]{:S(2)}, u32[]{:S(2)}) collective-permute-start(bf16[2,32,1536]{2,1,0:T(8,128)(2,1)S(1)} %bitcast.7), channel_id=1, source_target_pairs={{0,8},{4,12},{8,0},{12,4},{16,24},{20,28},{24,16},{28,20},{1,9},{5... | collective-permute-start | bytes 589832 | tf_op jit(solution)/shard_map/ppermute | solution.py:223
  24.5 9.6 %collective-permute-start.13 = (bf16[2,32,1536]{2,1,0:T(8,128)(2,1)S(1)}, bf16[2,32,1536]{2,1,0:T(8,128)(2,1)S(1)}, u32[]{:S(2)}, u32[]{:S(2)}) collective-permute-start(bf16[2,32,1536]{2,1,0:T(8,128)(2,1)S(1)} %bitcast.4), channel_id=1, source_target_pairs={{0,16},{4,20},{8,24},{12,28},{16,0},{20,4},{24,8},{28,12},{1,17},{... | collective-permute-start | bytes 589832 | tf_op jit(solution)/shard_map/ppermute | solution.py:223
  27.8 8.3 %collective-permute-start.10 = (bf16[2,2,32,768]{3,2,1,0:T(8,128)(2,1)S(1)}, bf16[2,2,32,768]{3,2,1,0:T(8,128)(2,1)S(1)}, u32[]{:S(2)}, u32[]{:S(2)}) collective-permute-start(bf16[2,2,32,768]{3,2,1,0:T(8,128)(2,1)S(1)} %get-tuple-element.37), channel_id=1, source_target_pairs={{0,1},{1,0},{2,3},{3,2},{4,5},{5,4},{6,7},{7,6},{8,9},{9,8},{10,11... | collective-permute-start | bytes 589832 | tf_op jit(solution)/shard_map/ppermute | solution.py:221
  29.7 8.2 %collective-permute-start.19 = (bf16[2,32,1536]{2,1,0:T(8,128)(2,1)S(1)}, bf16[2,32,1536]{2,1,0:T(8,128)(2,1)S(1)}, u32[]{:S(2)}, u32[]{:S(2)}) collective-permute-start(bf16[2,32,1536]{2,1,0:T(8,128)(2,1)S(1)} %collective-permute-done.9.low_ref), channel_id=1, source_target_pairs={{0,8},{4,12},{8,0},{12,4},{16,24},{20,28},{24,16},{28,20},{1,9},{5... | collective-permute-start | bytes 589832 | tf_op jit(solution)/shard_map/ppermute | solution.py:223
  30.5 7.4 %collective-permute-start.18 = (bf16[2,32,1536]{2,1,0:T(8,128)(2,1)S(1)}, bf16[2,32,1536]{2,1,0:T(8,128)(2,1)S(1)}, u32[]{:S(2)}, u32[]{:S(2)}) collective-permute-start(bf16[2,32,1536]{2,1,0:T(8,128)(2,1)S(1)} %collective-permute-done.8.high_ref), channel_id=1, source_target_pairs={{0,16},{4,20},{8,24},{12,28},{16,0},{20,4},{24,8},{28,12},{1,17},{... | collective-permute-start | bytes 589832 | tf_op jit(solution)/shard_map/ppermute | solution.py:223
  31.5 6.4 %collective-permute-start.7 = (bf16[2,32,768]{2,1,0:T(8,128)(2,1)S(1)}, bf16[2,32,768]{2,1,0:T(8,128)(2,1)S(1)}, u32[]{:S(2)}, u32[]{:S(2)}) collective-permute-start(bf16[2,32,768]{2,1,0:T(8,128)(2,1)S(1)} %get-tuple-element.35), channel_id=1, source_target_pairs={{0,2},{1,3},{2,0},{3,1},{4,6},{5,7},{6,4},{7,5},{8,10},{9,11},{10,... | collective-permute-start | bytes 294920 | tf_op jit(solution)/shard_map/ppermute | solution.py:307
  34.9 8.9 %collective-permute-start.15 = (bf16[2,2,32,768]{3,2,1,0:T(8,128)(2,1)S(1)}, bf16[2,2,32,768]{3,2,1,0:T(8,128)(2,1)S(1)}, u32[]{:S(2)}, u32[]{:S(2)}) collective-permute-start(bf16[2,2,32,768]{3,2,1,0:T(8,128)(2,1)S(1)} %get-tuple-element.41), channel_id=1, source_target_pairs={{0,1},{1,0},{2,3},{3,2},{4,5},{5,4},{6,7},{7,6},{8,9},{9,8},{10,11... | collective-permute-start | bytes 589832 | tf_op jit(solution)/shard_map/ppermute | solution.py:221
  38.7 10.7 %collective-permute-start.20 = (bf16[2,2,32,768]{3,2,1,0:T(8,128)(2,1)S(1)}, bf16[2,2,32,768]{3,2,1,0:T(8,128)(2,1)S(1)}, u32[]{:S(2)}, u32[]{:S(2)}) collective-permute-start(bf16[2,2,32,768]{3,2,1,0:T(8,128)(2,1)S(1)} %get-tuple-element.45), channel_id=1, source_target_pairs={{0,1},{1,0},{2,3},{3,2},{4,5},{5,4},{6,7},{7,6},{8,9},{9,8},{10,11... | collective-permute-start | bytes 589832 | tf_op jit(solution)/shard_map/ppermute | solution.py:221
  39.7 4.6 %collective-permute-start.12 = (bf16[2,32,768]{2,1,0:T(8,128)(2,1)S(1)}, bf16[2,32,768]{2,1,0:T(8,128)(2,1)S(1)}, u32[]{:S(2)}, u32[]{:S(2)}) collective-permute-start(bf16[2,32,768]{2,1,0:T(8,128)(2,1)S(1)} %get-tuple-element.40.refs_1_), channel_id=1, source_target_pairs={{0,16},{1,17},{2,10},{3,11},{4,20},{5,21},{6,14},{7,15},{8,24},{9,... | collective-permute-start | bytes 294920 | tf_op jit(solution)/shard_map/ppermute | solution.py:307
  40.6 11.1 %collective-permute-start.11 = (bf16[2,32,768]{2,1,0:T(8,128)(2,1)S(1)}, bf16[2,32,768]{2,1,0:T(8,128)(2,1)S(1)}, u32[]{:S(2)}, u32[]{:S(2)}) collective-permute-start(bf16[2,32,768]{2,1,0:T(8,128)(2,1)S(1)} %get-tuple-element.39), channel_id=1, source_target_pairs={{0,10},{1,11},{2,16},{3,17},{4,14},{5,15},{6,20},{7,21},{8,2},{9,3... | collective-permute-start | bytes 294920 | tf_op jit(solution)/shard_map/ppermute | solution.py:307
  44.4 8.4 %collective-permute-start.16 = (bf16[2,32,768]{2,1,0:T(8,128)(2,1)S(1)}, bf16[2,32,768]{2,1,0:T(8,128)(2,1)S(1)}, u32[]{:S(2)}, u32[]{:S(2)}) collective-permute-start(bf16[2,32,768]{2,1,0:T(8,128)(2,1)S(1)} %get-tuple-element.43), channel_id=1, source_target_pairs={{0,18},{1,19},{2,8},{3,9},{4,22},{5,23},{6,12},{7,13},{8,26},{9,27... | collective-permute-start | bytes 294920 | tf_op jit(solution)/shard_map/ppermute | solution.py:307
  47.4 5.4 %collective-permute-start.17 = (bf16[2,32,768]{2,1,0:T(8,128)(2,1)S(1)}, bf16[2,32,768]{2,1,0:T(8,128)(2,1)S(1)}, u32[]{:S(2)}, u32[]{:S(2)}) collective-permute-start(bf16[2,32,768]{2,1,0:T(8,128)(2,1)S(1)} %get-tuple-element.44), channel_id=1, source_target_pairs={{0,8},{1,9},{2,18},{3,19},{4,12},{5,13},{6,22},{7,23},{8,0},{9,1},... | collective-permute-start | bytes 294920 | tf_op jit(solution)/shard_map/ppermute | solution.py:307
  49.5 8.4 %collective-permute-start.21 = (bf16[2,32,768]{2,1,0:T(8,128)(2,1)S(1)}, bf16[2,32,768]{2,1,0:T(8,128)(2,1)S(1)}, u32[]{:S(2)}, u32[]{:S(2)}) collective-permute-start(bf16[2,32,768]{2,1,0:T(8,128)(2,1)S(1)} %get-tuple-element.47), channel_id=1, source_target_pairs={{0,26},{1,27},{2,24},{3,25},{4,30},{5,31},{6,28},{7,29},{8,18},{9,... | collective-permute-start | bytes 294920 | tf_op jit(solution)/shard_map/ppermute | solution.py:307
  49.8 8.1 %collective-permute-start.22 = (bf16[2,32,768]{2,1,0:T(8,128)(2,1)S(1)}, bf16[2,32,768]{2,1,0:T(8,128)(2,1)S(1)}, u32[]{:S(2)}, u32[]{:S(2)}) collective-permute-start(bf16[2,32,768]{2,1,0:T(8,128)(2,1)S(1)} %get-tuple-element.48), channel_id=1, source_target_pairs={{0,24},{1,25},{2,26},{3,27},{4,28},{5,29},{6,30},{7,31},{8,16},{9,... | collective-permute-start | bytes 294920 | tf_op jit(solution)/shard_map/ppermute | solution.py:307
where the time goes:
time: 59 us; the launch traced here: 58.8 us
  starting transfers between devices  34.1 us (58%)
  waiting for transfers between devices  14.7 us (25%)
  Pallas kernels  9.9 us (17%)
    ppermute x7, starting transfers between devices, owned(): return lax.ppermute(value, ('seq', 'head'), pairs)  14 us
    ppermute x11, starting transfers between devices, swap(): return lax.ppermute(value, 'seq', [(i, i ^ k) for i in range(seq)])  12.4 us
    ppermute x7, waiting for transfers between devices, owned(): return lax.ppermute(value, ('seq', 'head'), pairs)  8.48 us
    ppermute x11, waiting for transfers between devices, swap(): return lax.ppermute(value, 'seq', [(i, i ^ k) for i in range(seq)])  6.16 us
    ppermute x4, starting transfers between devices, swap(): return lax.ppermute(value, 'head', [(i, i ^ z) for i in range(groups)])  5.82 us
    pallas_call x4, Pallas kernels, projected(): pl.pallas_call(project_kernel, out_shape=(shaped(2, half, rows, wide),) *...  3.13 us
    pallas_call x1, Pallas kernels, local(): pl.pallas_call(turn_kernel, out_shape=shaped(2, feat, wide), in_specs=[hb...  2.35 us
    pallas_call x1, Pallas kernels, local(): pl.pallas_call(pick_kernel, out_shape=(shaped(2, per_block, feat), shaped...  2.05 us
  transfers between devices with their start and end apart: 23, of which 8 were waited for; matrix products, arithmetic and copies ran while one was open for 0% of the time, Pallas kernels for 14%

commit v1 on v0

--- a/solution.py
+++ b/solution.py
@@ -13,8 +13,6 @@
 NEGATIVE_FILL = -1e30
 LAST = (((1,), (1,)), ((), ()))
 BF16 = jnp.bfloat16
-BRIEF = pl.CostEstimate(flops=0, bytes_accessed=0, transcendentals=0)
-LONGER = pl.CostEstimate(flops=1_100_000_000, bytes_accessed=3_000_000, transcendentals=0)
 PARAMS = pltpu.CompilerParams(vmem_limit_bytes=32 << 20)
 
 
@@ -178,14 +176,33 @@
         ref[...] = total.astype(BF16)
 
 
+def split_both_kernel(first_came, first_keep, came_ref, keep_ref, *refs):
+    away_ref, *stay_refs = refs[-3:]
+    side = lax.axis_index("head") // 2
+    for n, (came, keep) in enumerate(((first_came, first_keep), (came_ref, keep_ref))):
+        away = came[:, side].astype(jnp.float32) + keep[:, side].astype(jnp.float32)
+        away_ref[n] = away.astype(BF16)
+        stay = came[:, 1 - side].astype(jnp.float32) + keep[:, 1 - side].astype(jnp.float32)
+        stay_refs[n][...] = stay.astype(BF16)
+
+
+def add_both_kernel(came_ref, *refs):
+    for n in range(2):
+        total = came_ref[n].astype(jnp.float32) + refs[n][...].astype(jnp.float32)
+        refs[2 + n][...] = total.astype(BF16)
+
+
 def join_kernel(chunks, *refs):
     out_ref = refs[-1]
     wide = refs[0].shape[-1]
     chip = lax.axis_index("seq") // 2
     upper = lax.axis_index("head") // 2
-    for n, (high, low) in enumerate(chunks):
-        total = refs[2 * n][...].astype(jnp.float32) + refs[2 * n + 1][...].astype(jnp.float32)
-        total = total.astype(BF16)
+    at = 0
+    for high, low, count in chunks:
+        total = refs[at][...]
+        if count == 2:
+            total = (total.astype(jnp.float32) + refs[at + 1][...].astype(jnp.float32)).astype(BF16)
+        at += count
         source = chip ^ (high if high == low else jnp.where(upper == 1, high, low))
         if len(out_ref.shape) == 4:
             out_ref[source] = total
@@ -195,14 +212,12 @@
             out_ref[:, pl.ds(start + c * wide, wide)] = total[c]
 
 
-def order_of_projection(n, keeps, stays, found):
-    if n == 3:
-        return [keeps[2], stays[1], found[0][0]]
-    return [keeps[n - 1]] if 0 < n < 3 else []
-
-
-def order_of_split(n, found):
-    return [found[1][1]] if n in (2, 3) else []
+def order_of_projection(n, keeps):
+    return [keeps[n - 1]] if 0 < n < 4 else []
+
+
+def order_of_split(n, stays, found):
+    return [found[0][0], stays[2]] if n == 3 else []
 
 
 def local(queries, keys, values, band, picks, w_out):
@@ -267,10 +282,9 @@
             in_specs=[vmem()] * (6 + len(behind)) + [pl.BlockSpec(memory_space=pl.ANY)] * len(order),
             out_specs=vmem(),
             compiler_params=PARAMS,
-            cost_estimate=LONGER,
         )(width, queries, keys, values, *behind, mine, other, *order).reshape(half, rows, feat)
 
-    highs = [attended(False, (), (halo, turned))]
+    highs = [attended(False, (), (halo, turned,))]
     lows = [attended(True, (halo,), (turned,))]
     for k in range(1, chips):
         if k == 3:
@@ -293,7 +307,6 @@
             in_specs=[vmem()] * 3 + specs,
             out_specs=(vmem(),) * 2,
             compiler_params=PARAMS,
-            cost_estimate=BRIEF,
         )(highs[high], lows[low], turned, *arrays)
 
     def owned(value, high, low, leaves):
@@ -306,24 +319,45 @@
                 pairs.append((s * groups + h, (s ^ 2 * k) * groups + (h ^ 2 * leaves)))
         return lax.ppermute(value, ("seq", "head"), pairs)
 
-    sends, keeps, aways, stays, found = {}, {}, {}, {}, {}
+    sends, keeps, cames, aways, stays, found = {}, {}, {}, {}, {}, {}
     for n, (high, low) in enumerate(chunks):
-        sends[n], keeps[n] = projected(high, low, order_of_projection(n, keeps, stays, found))
-        came = swap(sends[n], 0, 1)
-        specs, arrays = after(*order_of_split(n, found))
+        sends[n], keeps[n] = projected(high, low, order_of_projection(n, keeps))
+        cames[n] = swap(sends[n], 0, 1)
+        if n == 0 and chips > 1:
+            continue
+        specs, arrays = after(*order_of_split(n, stays, found))
+        if n == 1:
+            away, stays[0], stays[1] = pl.pallas_call(
+                split_both_kernel,
+                out_shape=(shaped(2, 2, rows, wide),) + (shaped(2, rows, wide),) * 2,
+                in_specs=[vmem()] * 4 + specs,
+                out_specs=(vmem(),) * 3,
+                compiler_params=PARAMS,
+            )(cames[0], keeps[0], cames[1], keeps[1], *arrays)
+            totals = pl.pallas_call(
+                add_both_kernel,
+                out_shape=(shaped(2, rows, wide),) * 2,
+                in_specs=[vmem()] * 3,
+                out_specs=(vmem(),) * 2,
+                compiler_params=PARAMS,
+            )(swap(away, 0, 2), stays[0], stays[1])
+            found[0], found[1] = [totals[0]], [owned(totals[1], high, low, False)]
+            continue
         aways[n], stays[n] = pl.pallas_call(
             split_kernel,
             out_shape=(shaped(2, rows, wide),) * 2,
             in_specs=[vmem()] * 2 + specs,
             out_specs=(vmem(),) * 2,
             compiler_params=PARAMS,
-        )(came, keeps[n], *arrays)
-        found[n] = (owned(aways[n], high, low, True), owned(stays[n], high, low, False))
+        )(cames[n], keeps[n], *arrays)
+        found[n] = [owned(aways[n], high, low, True), owned(stays[n], high, low, False)]
     flat = wide % 128 == 0
     joined = pl.pallas_call(
-        functools.partial(join_kernel, chunks),
+        functools.partial(
+            join_kernel, [(high, low, len(found[n])) for n, (high, low) in enumerate(chunks)]
+        ),
         out_shape=jax.ShapeDtypeStruct((rows, seq * wide) if flat else (chips, 2, rows, wide), BF16),
-        in_specs=[vmem()] * (2 * chips),
+        in_specs=[vmem()] * sum(len(pieces) for pieces in found.values()),
         out_specs=vmem(),
         compiler_params=PARAMS,
     )(*[piece for n in range(chips) for piece in found[n]])

time: 59 us -> 59.8 us (1.014)
  waiting for transfers between devices: 14.7 us -> 21.6 us
  starting transfers between devices: 34.1 us -> 28 us
    ppermute x4 -> x5, waiting for transfers between devices: 0.01 us -> 9.31 us  [swap(): return lax.ppermute(value, 'head', [(i, i ^ z) for i in range(groups)])]
    ppermute x7 -> x5, starting transfers between devices: 14 us -> 5.77 us  [owned(): return lax.ppermute(value, ('seq', 'head'), pairs)]
    ppermute x7 -> x5, waiting for transfers between devices: 8.48 us -> 5.75 us  [owned(): return lax.ppermute(value, ('seq', 'head'), pairs)]
    ppermute x4 -> x5, starting transfers between devices: 5.82 us -> 8.4 us  [swap(): return lax.ppermute(value, 'head', [(i, i ^ z) for i in range(groups)])]
  transfers between devices with their start and end apart: 23 -> 22, of which waited for: 8 -> 9; matrix products, arithmetic and copies ran while one was open for 0% -> 0% of each run, Pallas kernels for 14% -> 14%
where the time goes in v1:
time: 59.8 us; the launch traced here: 59.6 us
  starting transfers between devices  28 us (47%)
  waiting for transfers between devices  21.6 us (36%)
  Pallas kernels  9.92 us (17%)
    ppermute x11, starting transfers between devices, swap(): return lax.ppermute(value, 'seq', [(i, i ^ k) for i in range(seq)])  12 us
    ppermute x5, waiting for transfers between devices, swap(): return lax.ppermute(value, 'head', [(i, i ^ z) for i in range(groups)])  9.31 us
    ppermute x5, starting transfers between devices, swap(): return lax.ppermute(value, 'head', [(i, i ^ z) for i in range(groups)])  8.4 us
    ppermute x11, waiting for transfers between devices, swap(): return lax.ppermute(value, 'seq', [(i, i ^ k) for i in range(seq)])  6.49 us
    ppermute x5, starting transfers between devices, owned(): return lax.ppermute(value, ('seq', 'head'), pairs)  5.77 us
    ppermute x5, waiting for transfers between devices, owned(): return lax.ppermute(value, ('seq', 'head'), pairs)  5.75 us
    pallas_call x4, Pallas kernels, projected(): pl.pallas_call(project_kernel, out_shape=(shaped(2, half, rows, wide),) *...  3.13 us
    pallas_call x1, Pallas kernels, local(): pl.pallas_call(turn_kernel, out_shape=shaped(2, feat, wide), in_specs=[hb...  2.35 us
  transfers between devices with their start and end apart: 22, of which 9 were waited for; matrix products, arithmetic and copies ran while one was open for 0% of the time, Pallas kernels for 14%

profile of v1, /device:TPU:0, one launch (start us, length us, event | category | flops | bytes accessed | tf_op | source)
XLA Modules:
  0.0 59.6 jit_solution(12753889404515445321)
XLA Ops:
  0.0 0.5 collective-permute-start.5
  0.5 2.1 %shard_map.64 = (bf16[2,16,1536]{2,1,0:T(8,128)(2,1)S(1)}, bf16[2,64,1536]{2,1,0:T(8,128)(2,1)S(1)}, s32[12,256]{1,0:T(8,128)S(1)}, bf16[128,1536]{1,0:T(8,128)(...) custom-call(s32[1,16]{1,0:T(1,128)} %picks_ref.1, s32[12]{0:T(128)} %band_ref.1, ...), custom_call_target="tpu_custom_call" | custom-call | tf_op jit(solution)/shard_map/pallas_call | solution.py:246
  2.5 2.6 %collective-permute-start = (bf16[2,16,1536]{2,1,0:T(8,128)(2,1)S(1)}, bf16[2,16,1536]{2,1,0:T(8,128)(2,1)S(1)}, u32[]{:S(2)}, u32[]{:S(2)}) collective-permute-start(bf16[2,16,1536]{2,1,0:T(8,128)(2,1)S(1)} %get-tuple-element.32.refs_0_), channel_id=1, source_target_pairs={{0,8},{4,12},{8,0},{12,4},{16,24},{20,28},{24,16},{28,20},{1,9},{5... | collective-permute-start | bytes 294920 | tf_op jit(solution)/shard_map/ppermute | solution.py:238
  5.1 1.5 %collective-permute-start.1 = (bf16[2,16,1536]{2,1,0:T(8,128)(2,1)S(1)}, bf16[2,16,1536]{2,1,0:T(8,128)(2,1)S(1)}, u32[]{:S(2)}, u32[]{:S(2)}) collective-permute-start(bf16[2,16,1536]{2,1,0:T(8,128)(2,1)S(1)} %get-tuple-element.32.refs_0_), channel_id=1, source_target_pairs={{0,16},{4,20},{8,24},{12,28},{16,0},{20,4},{24,8},{28,12},{1,17},{... | collective-permute-start | bytes 294920 | tf_op jit(solution)/shard_map/ppermute | solution.py:238
  6.6 0.0 collective-permute-start.2
  6.6 1.9 %collective-permute-start.4 = (bf16[2,64,1536]{2,1,0:T(8,128)(2,1)S(1)}, bf16[2,64,1536]{2,1,0:T(8,128)(2,1)S(1)}, u32[]{:S(2)}, u32[]{:S(2)}) collective-permute-start(bf16[2,64,1536]{2,1,0:T(8,128)(2,1)S(1)} %get-tuple-element.33), channel_id=1, source_target_pairs={{0,4},{4,8},{8,12},{12,16},{16,20},{20,24},{24,28},{1,5},{5,9},{9,... | collective-permute-start | bytes 1179656 | tf_op jit(solution)/shard_map/ppermute | solution.py:260
  8.5 0.1 collective-permute-done.refs_1_
  8.5 2.6 %collective-permute-done.1.refs_2_ = bf16[2,16,1536]{2,1,0:T(8,128)(2,1)S(1)} collective-permute-done((bf16[2,16,1536]{2,1,0:T(8,128)(2,1)S(1)}, bf16[2,16,1536]{2,1,0:T(8,128)(2,1)S(1)}, u32[]{:S(2)}, u32[]{:S(2)}) %collective-permute-start.1) | collective-permute-done | bytes 98336 | tf_op jit(solution)/shard_map/ppermute | solution.py:238
  11.1 1.0 %collective-permute-done.2.refs_3_ = bf16[2,16,1536]{2,1,0:T(8,128)(2,1)S(1)} collective-permute-done((bf16[2,16,1536]{2,1,0:T(8,128)(2,1)S(1)}, bf16[2,16,1536]{2,1,0:T(8,128)(2,1)S(1)}, u32[]{:S(2)}, u32[]{:S(2)}) %collective-permute-start.2) | collective-permute-done | bytes 98336 | tf_op jit(solution)/shard_map/ppermute | solution.py:238
  12.2 0.1 collective-permute-start.3
  12.3 2.3 %shard_map.66.refs_3_.turned_ref = bf16[2,1536,768]{2,1,0:T(8,128)(2,1)S(1)} custom-call(bf16[768,1536]{1,0:T(8,128)(2,1)} %mine_hbm.1, bf16[768,1536]{1,0:T(8,128)(2,1)S(1)} %collective-permute-done.5.other_ref, bf16[4,2,16,1536]{3,2,1,0:T(8,128)(2,1)S(1)} %shard_map.65.order_ref.refs_0_.refs_1_), custom_call_target="tpu_custom_call" | custom-call | tf_op jit(solution)/shard_map/pallas_call | solution.py:269
  14.6 0.0 collective-permute-done.4.refs_2_.refs_0_
  14.6 0.0 collective-permute-done.3.refs_1_.refs_2_
  14.6 0.7 %shard_map.68 = bf16[64,1536]{1,0:T(8,128)(2,1)S(1)} custom-call(s32[12,256]{1,0:T(8,128)S(1)} %get-tuple-element.28.width_ref, bf16[128,1536]{1,0:T(8,128)(2,1)S(1)} %get-tuple-element.29.q_ref, bf16[128,1536]{1,0:T(8,128)(2,1)S(1)} %get-tuple-element.30.k_ref, bf16[128,1536]{1,0:T(8,128)(2,1)S(1)} %get-tuple-element.31.v_ref, ...), custom_call_target="tpu_custom_call" | custom-call | tf_op jit(solution)/shard_map/pallas_call | solution.py:279
  15.3 4.0 %collective-permute-start.8 = (bf16[2,32,1536]{2,1,0:T(8,128)(2,1)S(1)}, bf16[2,32,1536]{2,1,0:T(8,128)(2,1)S(1)}, u32[]{:S(2)}, u32[]{:S(2)}) collective-permute-start(bf16[2,32,1536]{2,1,0:T(8,128)(2,1)S(1)} %bitcast.5), channel_id=1, source_target_pairs={{0,16},{4,20},{8,24},{12,28},{16,0},{20,4},{24,8},{28,12},{1,17},{... | collective-permute-start | bytes 589832 | tf_op jit(solution)/shard_map/ppermute | solution.py:238
  19.3 0.7 %shard_map.67 = bf16[64,1536]{1,0:T(8,128)(2,1)S(1)} custom-call(s32[12,256]{1,0:T(8,128)S(1)} %get-tuple-element.28.width_ref, bf16[128,1536]{1,0:T(8,128)(2,1)S(1)} %get-tuple-element.29.q_ref, bf16[128,1536]{1,0:T(8,128)(2,1)S(1)} %get-tuple-element.30.k_ref, bf16[128,1536]{1,0:T(8,128)(2,1)S(1)} %get-tuple-element.31.v_ref, ...), custom_call_target="tpu_custom_call" | custom-call | tf_op jit(solution)/shard_map/pallas_call | solution.py:279
  20.0 0.7 %collective-permute-start.7 = (bf16[2,32,1536]{2,1,0:T(8,128)(2,1)S(1)}, bf16[2,32,1536]{2,1,0:T(8,128)(2,1)S(1)}, u32[]{:S(2)}, u32[]{:S(2)}) collective-permute-start(bf16[2,32,1536]{2,1,0:T(8,128)(2,1)S(1)} %bitcast.2), channel_id=1, source_target_pairs={{0,8},{4,12},{8,0},{12,4},{16,24},{20,28},{24,16},{28,20},{1,9},{5... | collective-permute-start | bytes 589832 | tf_op jit(solution)/shard_map/ppermute | solution.py:238
  20.6 1.4 %collective-permute-start.13 = (bf16[2,32,1536]{2,1,0:T(8,128)(2,1)S(1)}, bf16[2,32,1536]{2,1,0:T(8,128)(2,1)S(1)}, u32[]{:S(2)}, u32[]{:S(2)}) collective-permute-start(bf16[2,32,1536]{2,1,0:T(8,128)(2,1)S(1)} %bitcast.6), channel_id=1, source_target_pairs={{0,8},{4,12},{8,0},{12,4},{16,24},{20,28},{24,16},{28,20},{1,9},{5... | collective-permute-start | bytes 589832 | tf_op jit(solution)/shard_map/ppermute | solution.py:238
  22.1 0.8 %shard_map.69 = (bf16[2,2,32,768]{3,2,1,0:T(8,128)(2,1)S(1)}, bf16[2,2,32,768]{3,2,1,0:T(8,128)(2,1)S(1)}) custom-call(bf16[2,32,1536]{2,1,0:T(8,128)(2,1)S(1)} %bitcast.3, bf16[2,32,1536]{2,1,0:T(8,128)(2,1)S(1)} %bitcast.7, bf16[2,1536,768]{2,1,0:T(8,128)(2,1)S(1)} %shard_map.66.refs_3_.turned_ref), custom_call_target="tpu_custom_call" | custom-call | tf_op jit(solution)/shard_map/pallas_call | solution.py:304
  22.8 0.1 collective-permute-start.12
  22.9 1.6 %collective-permute-start.6 = (bf16[2,2,32,768]{3,2,1,0:T(8,128)(2,1)S(1)}, bf16[2,2,32,768]{3,2,1,0:T(8,128)(2,1)S(1)}, u32[]{:S(2)}, u32[]{:S(2)}) collective-permute-start(bf16[2,2,32,768]{3,2,1,0:T(8,128)(2,1)S(1)} %get-tuple-element.34), channel_id=1, source_target_pairs={{0,1},{1,0},{2,3},{3,2},{4,5},{5,4},{6,7},{7,6},{8,9},{9,8},{10,11... | collective-permute-start | bytes 589832 | tf_op jit(solution)/shard_map/ppermute | solution.py:236
  24.6 0.0 collective-permute-done.8.low_ref
  24.6 2.3 %collective-permute-done.7.high_ref = bf16[2,32,1536]{2,1,0:T(8,128)(2,1)S(1)} collective-permute-done((bf16[2,32,1536]{2,1,0:T(8,128)(2,1)S(1)}, bf16[2,32,1536]{2,1,0:T(8,128)(2,1)S(1)}, u32[]{:S(2)}, u32[]{:S(2)}) %collective-permute-start.7) | collective-permute-done | bytes 196640 | tf_op jit(solution)/shard_map/ppermute | solution.py:238
  26.9 0.8 %shard_map.70 = (bf16[2,2,32,768]{3,2,1,0:T(8,128)(2,1)S(1)}, bf16[2,2,32,768]{3,2,1,0:T(8,128)(2,1)S(1)}) custom-call(bf16[2,32,1536]{2,1,0:T(8,128)(2,1)S(1)} %collective-permute-done.7.high_ref, bf16[2,32,1536]{2,1,0:T(8,128)(2,1)S(1)} %collective-permute-done.8.low_ref, bf16[2,1536,768]{2,1,0:T(8,128)(2,1)S(1)} %shard_map.66.refs_3_.turned_ref, ...), custom_call_target="tpu_custom_call" | custom-call | tf_op jit(solution)/shard_map/pallas_call | solution.py:304
  27.7 2.1 %collective-permute-start.9 = (bf16[2,2,32,768]{3,2,1,0:T(8,128)(2,1)S(1)}, bf16[2,2,32,768]{3,2,1,0:T(8,128)(2,1)S(1)}, u32[]{:S(2)}, u32[]{:S(2)}) collective-permute-start(bf16[2,2,32,768]{3,2,1,0:T(8,128)(2,1)S(1)} %get-tuple-element.36), channel_id=1, source_target_pairs={{0,1},{1,0},{2,3},{3,2},{4,5},{5,4},{6,7},{7,6},{8,9},{9,8},{10,11... | collective-permute-start | bytes 589832 | tf_op jit(solution)/shard_map/ppermute | solution.py:236
  29.7 0.2 collective-permute-start.18
  29.9 0.5 collective-permute-done.13.low_ref
  30.4 1.0 %collective-permute-start.17 = (bf16[2,32,1536]{2,1,0:T(8,128)(2,1)S(1)}, bf16[2,32,1536]{2,1,0:T(8,128)(2,1)S(1)}, u32[]{:S(2)}, u32[]{:S(2)}) collective-permute-start(bf16[2,32,1536]{2,1,0:T(8,128)(2,1)S(1)} %collective-permute-done.7.high_ref), channel_id=1, source_target_pairs={{0,16},{4,20},{8,24},{12,28},{16,0},{20,4},{24,8},{28,12},{1,17},{... | collective-permute-start | bytes 589832 | tf_op jit(solution)/shard_map/ppermute | solution.py:238
  31.4 0.8 %shard_map.73 = (bf16[2,2,32,768]{3,2,1,0:T(8,128)(2,1)S(1)}, bf16[2,2,32,768]{3,2,1,0:T(8,128)(2,1)S(1)}) custom-call(bf16[2,32,1536]{2,1,0:T(8,128)(2,1)S(1)} %collective-permute-done.12.high_ref, bf16[2,32,1536]{2,1,0:T(8,128)(2,1)S(1)} %collective-permute-done.13.low_ref, bf16[2,1536,768]{2,1,0:T(8,128)(2,1)S(1)} %shard_map.66.refs_3_.turned_ref, ...), custom_call_target="tpu_custom_call" | custom-call | tf_op jit(solution)/shard_map/pallas_call | solution.py:304
  32.2 1.8 %collective-permute-start.14 = (bf16[2,2,32,768]{3,2,1,0:T(8,128)(2,1)S(1)}, bf16[2,2,32,768]{3,2,1,0:T(8,128)(2,1)S(1)}, u32[]{:S(2)}, u32[]{:S(2)}) collective-permute-start(bf16[2,2,32,768]{3,2,1,0:T(8,128)(2,1)S(1)} %get-tuple-element.43), channel_id=1, source_target_pairs={{0,1},{1,0},{2,3},{3,2},{4,5},{5,4},{6,7},{7,6},{8,9},{9,8},{10,11... | collective-permute-start | bytes 589832 | tf_op jit(solution)/shard_map/ppermute | solution.py:236
  34.0 3.2 %collective-permute-done.9.came_ref = bf16[2,2,32,768]{3,2,1,0:T(8,128)(2,1)S(1)} collective-permute-done((bf16[2,2,32,768]{3,2,1,0:T(8,128)(2,1)S(1)}, bf16[2,2,32,768]{3,2,1,0:T(8,128)(2,1)S(1)}, u32[]{:S(2)}, u32[]{:S(2)}) %collective-permute-start.9) | collective-permute-done | bytes 196640 | tf_op jit(solution)/shard_map/ppermute | solution.py:236
  37.2 0.1 shard_map.71
  37.3 1.0 %collective-permute-start.10 = (bf16[2,2,32,768]{3,2,1,0:T(8,128)(2,1)S(1)}, bf16[2,2,32,768]{3,2,1,0:T(8,128)(2,1)S(1)}, u32[]{:S(2)}, u32[]{:S(2)}) collective-permute-start(bf16[2,2,32,768]{3,2,1,0:T(8,128)(2,1)S(1)} %get-tuple-element.38), channel_id=1, source_target_pairs={{0,2},{1,3},{2,0},{3,1},{4,6},{5,7},{6,4},{7,5},{8,10},{9,11},{10,... | collective-permute-start | bytes 589832 | tf_op jit(solution)/shard_map/ppermute | solution.py:236
  38.3 0.0 collective-permute-done.18.low_ref
  38.3 0.0 collective-permute-done.17.high_ref
  38.3 0.8 %shard_map.75 = (bf16[2,2,32,768]{3,2,1,0:T(8,128)(2,1)S(1)}, bf16[2,2,32,768]{3,2,1,0:T(8,128)(2,1)S(1)}) custom-call(bf16[2,32,1536]{2,1,0:T(8,128)(2,1)S(1)} %collective-permute-done.17.high_ref, bf16[2,32,1536]{2,1,0:T(8,128)(2,1)S(1)} %collective-permute-done.18.low_ref, bf16[2,1536,768]{2,1,0:T(8,128)(2,1)S(1)} %shard_map.66.refs_3_.turned_ref, ...), custom_call_target="tpu_custom_call" | custom-call | tf_op jit(solution)/shard_map/pallas_call | solution.py:304
  39.1 1.9 %collective-permute-start.19 = (bf16[2,2,32,768]{3,2,1,0:T(8,128)(2,1)S(1)}, bf16[2,2,32,768]{3,2,1,0:T(8,128)(2,1)S(1)}, u32[]{:S(2)}, u32[]{:S(2)}) collective-permute-start(bf16[2,2,32,768]{3,2,1,0:T(8,128)(2,1)S(1)} %get-tuple-element.47), channel_id=1, source_target_pairs={{0,1},{1,0},{2,3},{3,2},{4,5},{5,4},{6,7},{7,6},{8,9},{9,8},{10,11... | collective-permute-start | bytes 589832 | tf_op jit(solution)/shard_map/ppermute | solution.py:236
  41.0 0.0 collective-permute-done.14.came_ref
  41.1 3.0 %collective-permute-start.15 = (bf16[2,32,768]{2,1,0:T(8,128)(2,1)S(1)}, bf16[2,32,768]{2,1,0:T(8,128)(2,1)S(1)}, u32[]{:S(2)}, u32[]{:S(2)}) collective-permute-start(bf16[2,32,768]{2,1,0:T(8,128)(2,1)S(1)} %get-tuple-element.45), channel_id=1, source_target_pairs={{0,18},{1,19},{2,8},{3,9},{4,22},{5,23},{6,12},{7,13},{8,26},{9,27... | collective-permute-start | bytes 294920 | tf_op jit(solution)/shard_map/ppermute | solution.py:320
  44.0 0.8 %collective-permute-start.16 = (bf16[2,32,768]{2,1,0:T(8,128)(2,1)S(1)}, bf16[2,32,768]{2,1,0:T(8,128)(2,1)S(1)}, u32[]{:S(2)}, u32[]{:S(2)}) collective-permute-start(bf16[2,32,768]{2,1,0:T(8,128)(2,1)S(1)} %get-tuple-element.46.refs_1_), channel_id=1, source_target_pairs={{0,8},{1,9},{2,18},{3,19},{4,12},{5,13},{6,22},{7,23},{8,0},{9,1},... | collective-permute-start | bytes 294920 | tf_op jit(solution)/shard_map/ppermute | solution.py:320
  44.8 6.1 %collective-permute-done.10.came_ref = bf16[2,2,32,768]{3,2,1,0:T(8,128)(2,1)S(1)} collective-permute-done((bf16[2,2,32,768]{3,2,1,0:T(8,128)(2,1)S(1)}, bf16[2,2,32,768]{3,2,1,0:T(8,128)(2,1)S(1)}, u32[]{:S(2)}, u32[]{:S(2)}) %collective-permute-start.10) | collective-permute-done | bytes 196640 | tf_op jit(solution)/shard_map/ppermute | solution.py:236
  51.0 0.1 shard_map.76
  51.1 0.1 collective-permute-start.20
  51.2 1.9 %collective-permute-start.21 = (bf16[2,32,768]{2,1,0:T(8,128)(2,1)S(1)}, bf16[2,32,768]{2,1,0:T(8,128)(2,1)S(1)}, u32[]{:S(2)}, u32[]{:S(2)}) collective-permute-start(bf16[2,32,768]{2,1,0:T(8,128)(2,1)S(1)} %get-tuple-element.50), channel_id=1, source_target_pairs={{0,24},{1,25},{2,26},{3,27},{4,28},{5,29},{6,30},{7,31},{8,16},{9,... | collective-permute-start | bytes 294920 | tf_op jit(solution)/shard_map/ppermute | solution.py:320
  53.1 0.0 collective-permute-done.15.refs_2_
  53.1 5.5 %collective-permute-done.20.refs_4_ = bf16[2,32,768]{2,1,0:T(8,128)(2,1)S(1)} collective-permute-done((bf16[2,32,768]{2,1,0:T(8,128)(2,1)S(1)}, bf16[2,32,768]{2,1,0:T(8,128)(2,1)S(1)}, u32[]{:S(2)}, u32[]{:S(2)}) %collective-permute-start.20) | collective-permute-done | bytes 98336 | tf_op jit(solution)/shard_map/ppermute | solution.py:320
  58.6 0.3 collective-permute-done.11.refs_1_
  58.8 0.8 %shard_map.77 = bf16[32,6144]{1,0:T(8,128)(2,1)} custom-call(bf16[2,32,768]{2,1,0:T(8,128)(2,1)S(1)} %get-tuple-element.41.refs_0_, bf16[2,32,768]{2,1,0:T(8,128)(2,1)S(1)} %collective-permute-done.11.refs_1_, bf16[2,32,768]{2,1,0:T(8,128)(2,1)S(1)} %collective-permute-done.15.refs_2_, bf16[2,32,768]{2,1,0:T(8,128)(2,1)S(1)} %collective-permute-done.16.refs_3_, ...), custom_call_target="tpu_custom_call" | custom-call | tf_op jit(solution)/shard_map/pallas_call | solution.py:355
  (10 shorter events, 0.1 us)
Async XLA Ops:
  0.0 12.2 %collective-permute-start.5 = (bf16[768,1536]{1,0:T(8,128)(2,1)}, bf16[768,1536]{1,0:T(8,128)(2,1)S(1)}, u32[]{:S(2)}, u32[]{:S(2)}) collective-permute-start(bf16[768,1536]{1,0:T(8,128)(2,1)} %mine_hbm.1), channel_id=1, source_target_pairs={{0,4},{4,0},{8,12},{12,8},{16,20},{20,16},{24,28},{28,24},{1,5},{5... | collective-permute-start | bytes 7077896 | tf_op jit(solution)/shard_map/ppermute | solution.py:238
  2.5 6.0 %collective-permute-start = (bf16[2,16,1536]{2,1,0:T(8,128)(2,1)S(1)}, bf16[2,16,1536]{2,1,0:T(8,128)(2,1)S(1)}, u32[]{:S(2)}, u32[]{:S(2)}) collective-permute-start(bf16[2,16,1536]{2,1,0:T(8,128)(2,1)S(1)} %get-tuple-element.32.refs_0_), channel_id=1, source_target_pairs={{0,8},{4,12},{8,0},{12,4},{16,24},{20,28},{24,16},{28,20},{1,9},{5... | collective-permute-start | bytes 294920 | tf_op jit(solution)/shard_map/ppermute | solution.py:238
  5.1 6.1 %collective-permute-start.1 = (bf16[2,16,1536]{2,1,0:T(8,128)(2,1)S(1)}, bf16[2,16,1536]{2,1,0:T(8,128)(2,1)S(1)}, u32[]{:S(2)}, u32[]{:S(2)}) collective-permute-start(bf16[2,16,1536]{2,1,0:T(8,128)(2,1)S(1)} %get-tuple-element.32.refs_0_), channel_id=1, source_target_pairs={{0,16},{4,20},{8,24},{12,28},{16,0},{20,4},{24,8},{28,12},{1,17},{... | collective-permute-start | bytes 294920 | tf_op jit(solution)/shard_map/ppermute | solution.py:238
  6.6 5.5 %collective-permute-start.2 = (bf16[2,16,1536]{2,1,0:T(8,128)(2,1)S(1)}, bf16[2,16,1536]{2,1,0:T(8,128)(2,1)S(1)}, u32[]{:S(2)}, u32[]{:S(2)}) collective-permute-start(bf16[2,16,1536]{2,1,0:T(8,128)(2,1)S(1)} %get-tuple-element.32.refs_0_), channel_id=1, source_target_pairs={{0,24},{4,28},{8,16},{12,20},{16,8},{20,12},{24,0},{28,4},{1,25},{... | collective-permute-start | bytes 294920 | tf_op jit(solution)/shard_map/ppermute | solution.py:238
  6.6 8.0 %collective-permute-start.4 = (bf16[2,64,1536]{2,1,0:T(8,128)(2,1)S(1)}, bf16[2,64,1536]{2,1,0:T(8,128)(2,1)S(1)}, u32[]{:S(2)}, u32[]{:S(2)}) collective-permute-start(bf16[2,64,1536]{2,1,0:T(8,128)(2,1)S(1)} %get-tuple-element.33), channel_id=1, source_target_pairs={{0,4},{4,8},{8,12},{12,16},{16,20},{20,24},{24,28},{1,5},{5,9},{9,... | collective-permute-start | bytes 1179656 | tf_op jit(solution)/shard_map/ppermute | solution.py:260
  12.2 2.5 %collective-permute-start.3 = (bf16[4,2,16,1536]{3,2,1,0:T(8,128)(2,1)S(1)}, bf16[4,2,16,1536]{3,2,1,0:T(8,128)(2,1)S(1)}, u32[]{:S(2)}, u32[]{:S(2)}) collective-permute-start(bf16[4,2,16,1536]{3,2,1,0:T(8,128)(2,1)S(1)} %shard_map.65.order_ref.refs_0_.refs_1_), channel_id=1, source_target_pairs={{0,4},{4,0},{8,12},{12,8},{16,20},{20,16},{24,28},{28,24},{1,5},{5... | collective-permute-start | bytes 1179656 | tf_op jit(solution)/shard_map/ppermute | solution.py:238
  15.3 9.3 %collective-permute-start.8 = (bf16[2,32,1536]{2,1,0:T(8,128)(2,1)S(1)}, bf16[2,32,1536]{2,1,0:T(8,128)(2,1)S(1)}, u32[]{:S(2)}, u32[]{:S(2)}) collective-permute-start(bf16[2,32,1536]{2,1,0:T(8,128)(2,1)S(1)} %bitcast.5), channel_id=1, source_target_pairs={{0,16},{4,20},{8,24},{12,28},{16,0},{20,4},{24,8},{28,12},{1,17},{... | collective-permute-start | bytes 589832 | tf_op jit(solution)/shard_map/ppermute | solution.py:238
  20.0 6.9 %collective-permute-start.7 = (bf16[2,32,1536]{2,1,0:T(8,128)(2,1)S(1)}, bf16[2,32,1536]{2,1,0:T(8,128)(2,1)S(1)}, u32[]{:S(2)}, u32[]{:S(2)}) collective-permute-start(bf16[2,32,1536]{2,1,0:T(8,128)(2,1)S(1)} %bitcast.2), channel_id=1, source_target_pairs={{0,8},{4,12},{8,0},{12,4},{16,24},{20,28},{24,16},{28,20},{1,9},{5... | collective-permute-start | bytes 589832 | tf_op jit(solution)/shard_map/ppermute | solution.py:238
  20.6 9.8 %collective-permute-start.13 = (bf16[2,32,1536]{2,1,0:T(8,128)(2,1)S(1)}, bf16[2,32,1536]{2,1,0:T(8,128)(2,1)S(1)}, u32[]{:S(2)}, u32[]{:S(2)}) collective-permute-start(bf16[2,32,1536]{2,1,0:T(8,128)(2,1)S(1)} %bitcast.6), channel_id=1, source_target_pairs={{0,8},{4,12},{8,0},{12,4},{16,24},{20,28},{24,16},{28,20},{1,9},{5... | collective-permute-start | bytes 589832 | tf_op jit(solution)/shard_map/ppermute | solution.py:238
  22.8 8.6 %collective-permute-start.12 = (bf16[2,32,1536]{2,1,0:T(8,128)(2,1)S(1)}, bf16[2,32,1536]{2,1,0:T(8,128)(2,1)S(1)}, u32[]{:S(2)}, u32[]{:S(2)}) collective-permute-start(bf16[2,32,1536]{2,1,0:T(8,128)(2,1)S(1)} %bitcast.4), channel_id=1, source_target_pairs={{0,16},{4,20},{8,24},{12,28},{16,0},{20,4},{24,8},{28,12},{1,17},{... | collective-permute-start | bytes 589832 | tf_op jit(solution)/shard_map/ppermute | solution.py:238
  22.9 11.1 %collective-permute-start.6 = (bf16[2,2,32,768]{3,2,1,0:T(8,128)(2,1)S(1)}, bf16[2,2,32,768]{3,2,1,0:T(8,128)(2,1)S(1)}, u32[]{:S(2)}, u32[]{:S(2)}) collective-permute-start(bf16[2,2,32,768]{3,2,1,0:T(8,128)(2,1)S(1)} %get-tuple-element.34), channel_id=1, source_target_pairs={{0,1},{1,0},{2,3},{3,2},{4,5},{5,4},{6,7},{7,6},{8,9},{9,8},{10,11... | collective-permute-start | bytes 589832 | tf_op jit(solution)/shard_map/ppermute | solution.py:236
  27.7 9.6 %collective-permute-start.9 = (bf16[2,2,32,768]{3,2,1,0:T(8,128)(2,1)S(1)}, bf16[2,2,32,768]{3,2,1,0:T(8,128)(2,1)S(1)}, u32[]{:S(2)}, u32[]{:S(2)}) collective-permute-start(bf16[2,2,32,768]{3,2,1,0:T(8,128)(2,1)S(1)} %get-tuple-element.36), channel_id=1, source_target_pairs={{0,1},{1,0},{2,3},{3,2},{4,5},{5,4},{6,7},{7,6},{8,9},{9,8},{10,11... | collective-permute-start | bytes 589832 | tf_op jit(solution)/shard_map/ppermute | solution.py:236
  29.7 8.6 %collective-permute-start.18 = (bf16[2,32,1536]{2,1,0:T(8,128)(2,1)S(1)}, bf16[2,32,1536]{2,1,0:T(8,128)(2,1)S(1)}, u32[]{:S(2)}, u32[]{:S(2)}) collective-permute-start(bf16[2,32,1536]{2,1,0:T(8,128)(2,1)S(1)} %collective-permute-done.8.low_ref), channel_id=1, source_target_pairs={{0,8},{4,12},{8,0},{12,4},{16,24},{20,28},{24,16},{28,20},{1,9},{5... | collective-permute-start | bytes 589832 | tf_op jit(solution)/shard_map/ppermute | solution.py:238
  30.4 7.9 %collective-permute-start.17 = (bf16[2,32,1536]{2,1,0:T(8,128)(2,1)S(1)}, bf16[2,32,1536]{2,1,0:T(8,128)(2,1)S(1)}, u32[]{:S(2)}, u32[]{:S(2)}) collective-permute-start(bf16[2,32,1536]{2,1,0:T(8,128)(2,1)S(1)} %collective-permute-done.7.high_ref), channel_id=1, source_target_pairs={{0,16},{4,20},{8,24},{12,28},{16,0},{20,4},{24,8},{28,12},{1,17},{... | collective-permute-start | bytes 589832 | tf_op jit(solution)/shard_map/ppermute | solution.py:238
  32.2 8.8 %collective-permute-start.14 = (bf16[2,2,32,768]{3,2,1,0:T(8,128)(2,1)S(1)}, bf16[2,2,32,768]{3,2,1,0:T(8,128)(2,1)S(1)}, u32[]{:S(2)}, u32[]{:S(2)}) collective-permute-start(bf16[2,2,32,768]{3,2,1,0:T(8,128)(2,1)S(1)} %get-tuple-element.43), channel_id=1, source_target_pairs={{0,1},{1,0},{2,3},{3,2},{4,5},{5,4},{6,7},{7,6},{8,9},{9,8},{10,11... | collective-permute-start | bytes 589832 | tf_op jit(solution)/shard_map/ppermute | solution.py:236
  37.3 13.6 %collective-permute-start.10 = (bf16[2,2,32,768]{3,2,1,0:T(8,128)(2,1)S(1)}, bf16[2,2,32,768]{3,2,1,0:T(8,128)(2,1)S(1)}, u32[]{:S(2)}, u32[]{:S(2)}) collective-permute-start(bf16[2,2,32,768]{3,2,1,0:T(8,128)(2,1)S(1)} %get-tuple-element.38), channel_id=1, source_target_pairs={{0,2},{1,3},{2,0},{3,1},{4,6},{5,7},{6,4},{7,5},{8,10},{9,11},{10,... | collective-permute-start | bytes 589832 | tf_op jit(solution)/shard_map/ppermute | solution.py:236
  39.1 11.9 %collective-permute-start.19 = (bf16[2,2,32,768]{3,2,1,0:T(8,128)(2,1)S(1)}, bf16[2,2,32,768]{3,2,1,0:T(8,128)(2,1)S(1)}, u32[]{:S(2)}, u32[]{:S(2)}) collective-permute-start(bf16[2,2,32,768]{3,2,1,0:T(8,128)(2,1)S(1)} %get-tuple-element.47), channel_id=1, source_target_pairs={{0,1},{1,0},{2,3},{3,2},{4,5},{5,4},{6,7},{7,6},{8,9},{9,8},{10,11... | collective-permute-start | bytes 589832 | tf_op jit(solution)/shard_map/ppermute | solution.py:236
  41.1 12.0 %collective-permute-start.15 = (bf16[2,32,768]{2,1,0:T(8,128)(2,1)S(1)}, bf16[2,32,768]{2,1,0:T(8,128)(2,1)S(1)}, u32[]{:S(2)}, u32[]{:S(2)}) collective-permute-start(bf16[2,32,768]{2,1,0:T(8,128)(2,1)S(1)} %get-tuple-element.45), channel_id=1, source_target_pairs={{0,18},{1,19},{2,8},{3,9},{4,22},{5,23},{6,12},{7,13},{8,26},{9,27... | collective-permute-start | bytes 294920 | tf_op jit(solution)/shard_map/ppermute | solution.py:320
  44.0 9.1 %collective-permute-start.16 = (bf16[2,32,768]{2,1,0:T(8,128)(2,1)S(1)}, bf16[2,32,768]{2,1,0:T(8,128)(2,1)S(1)}, u32[]{:S(2)}, u32[]{:S(2)}) collective-permute-start(bf16[2,32,768]{2,1,0:T(8,128)(2,1)S(1)} %get-tuple-element.46.refs_1_), channel_id=1, source_target_pairs={{0,8},{1,9},{2,18},{3,19},{4,12},{5,13},{6,22},{7,23},{8,0},{9,1},... | collective-permute-start | bytes 294920 | tf_op jit(solution)/shard_map/ppermute | solution.py:320
  51.1 7.5 %collective-permute-start.20 = (bf16[2,32,768]{2,1,0:T(8,128)(2,1)S(1)}, bf16[2,32,768]{2,1,0:T(8,128)(2,1)S(1)}, u32[]{:S(2)}, u32[]{:S(2)}) collective-permute-start(bf16[2,32,768]{2,1,0:T(8,128)(2,1)S(1)} %get-tuple-element.49), channel_id=1, source_target_pairs={{0,26},{1,27},{2,24},{3,25},{4,30},{5,31},{6,28},{7,29},{8,18},{9,... | collective-permute-start | bytes 294920 | tf_op jit(solution)/shard_map/ppermute | solution.py:320
  51.2 7.4 %collective-permute-start.21 = (bf16[2,32,768]{2,1,0:T(8,128)(2,1)S(1)}, bf16[2,32,768]{2,1,0:T(8,128)(2,1)S(1)}, u32[]{:S(2)}, u32[]{:S(2)}) collective-permute-start(bf16[2,32,768]{2,1,0:T(8,128)(2,1)S(1)} %get-tuple-element.50), channel_id=1, source_target_pairs={{0,24},{1,25},{2,26},{3,27},{4,28},{5,29},{6,30},{7,31},{8,16},{9,... | collective-permute-start | bytes 294920 | tf_op jit(solution)/shard_map/ppermute | solution.py:320
  53.1 5.8 %collective-permute-start.11 = (bf16[2,32,768]{2,1,0:T(8,128)(2,1)S(1)}, bf16[2,32,768]{2,1,0:T(8,128)(2,1)S(1)}, u32[]{:S(2)}, u32[]{:S(2)}) collective-permute-start(bf16[2,32,768]{2,1,0:T(8,128)(2,1)S(1)} %get-tuple-element.42), channel_id=1, source_target_pairs={{0,16},{1,17},{2,10},{3,11},{4,20},{5,21},{6,14},{7,15},{8,24},{9,... | collective-permute-start | bytes 294920 | tf_op jit(solution)/shard_map/ppermute | solution.py:320

commit v2 on v0

--- a/solution.py
+++ b/solution.py
@@ -202,7 +202,7 @@
 
 
 def order_of_split(n, found):
-    return [found[1][1]] if n in (2, 3) else []
+    return [found[1][0]] if n == 3 else []
 
 
 def local(queries, keys, values, band, picks, w_out):

time: 59 us -> 58.1 us (0.985)
  waiting for transfers between devices: 14.7 us -> 11.3 us
  starting transfers between devices: 34.1 us -> 36.1 us
    ppermute x7, waiting for transfers between devices: 8.48 us -> 5.17 us  [owned(): return lax.ppermute(value, ('seq', 'head'), pairs)]
    ppermute x7, starting transfers between devices: 14 us -> 16 us  [owned(): return lax.ppermute(value, ('seq', 'head'), pairs)]
  transfers between devices with their start and end apart: 23 -> 23, of which waited for: 8 -> 7; matrix products, arithmetic and copies ran while one was open for 0% -> 0% of each run, Pallas kernels for 14% -> 15%
where the time goes in v2:
time: 58.1 us; the launch traced here: 57.5 us
  starting transfers between devices  36.1 us (62%)
  waiting for transfers between devices  11.3 us (19%)
  Pallas kernels  9.89 us (17%)
    ppermute x7, starting transfers between devices, owned(): return lax.ppermute(value, ('seq', 'head'), pairs)  16 us
    ppermute x11, starting transfers between devices, swap(): return lax.ppermute(value, 'seq', [(i, i ^ k) for i in range(seq)])  12.4 us
    ppermute x11, waiting for transfers between devices, swap(): return lax.ppermute(value, 'seq', [(i, i ^ k) for i in range(seq)])  6.16 us
    ppermute x4, starting transfers between devices, swap(): return lax.ppermute(value, 'head', [(i, i ^ z) for i in range(groups)])  5.78 us
    ppermute x7, waiting for transfers between devices, owned(): return lax.ppermute(value, ('seq', 'head'), pairs)  5.17 us
    pallas_call x4, Pallas kernels, projected(): pl.pallas_call(project_kernel, out_shape=(shaped(2, half, rows, wide),) *...  3.13 us
    pallas_call x1, Pallas kernels, local(): pl.pallas_call(turn_kernel, out_shape=shaped(2, feat, wide), in_specs=[hb...  2.35 us
    pallas_call x1, Pallas kernels, local(): pl.pallas_call(pick_kernel, out_shape=(shaped(2, per_block, feat), shaped...  2.05 us
  transfers between devices with their start and end apart: 23, of which 7 were waited for; matrix products, arithmetic and copies ran while one was open for 0% of the time, Pallas kernels for 15%

profile of v2, /device:TPU:0, one launch (start us, length us, event | category | flops | bytes accessed | tf_op | source)
XLA Modules:
  0.0 57.5 jit_solution(7268134564626956579)
XLA Ops:
  0.0 0.5 collective-permute-start.5
  0.5 2.1 %shard_map.64 = (bf16[2,16,1536]{2,1,0:T(8,128)(2,1)S(1)}, bf16[2,64,1536]{2,1,0:T(8,128)(2,1)S(1)}, s32[12,256]{1,0:T(8,128)S(1)}, bf16[128,1536]{1,0:T(8,128)(...) custom-call(s32[1,16]{1,0:T(1,128)} %picks_ref.1, s32[12]{0:T(128)} %band_ref.1, ...), custom_call_target="tpu_custom_call" | custom-call | tf_op jit(solution)/shard_map/pallas_call | solution.py:231
  2.5 2.6 %collective-permute-start = (bf16[2,16,1536]{2,1,0:T(8,128)(2,1)S(1)}, bf16[2,16,1536]{2,1,0:T(8,128)(2,1)S(1)}, u32[]{:S(2)}, u32[]{:S(2)}) collective-permute-start(bf16[2,16,1536]{2,1,0:T(8,128)(2,1)S(1)} %get-tuple-element.31.refs_0_), channel_id=1, source_target_pairs={{0,8},{4,12},{8,0},{12,4},{16,24},{20,28},{24,16},{28,20},{1,9},{5... | collective-permute-start | bytes 294920 | tf_op jit(solution)/shard_map/ppermute | solution.py:223
  5.1 1.5 %collective-permute-start.1 = (bf16[2,16,1536]{2,1,0:T(8,128)(2,1)S(1)}, bf16[2,16,1536]{2,1,0:T(8,128)(2,1)S(1)}, u32[]{:S(2)}, u32[]{:S(2)}) collective-permute-start(bf16[2,16,1536]{2,1,0:T(8,128)(2,1)S(1)} %get-tuple-element.31.refs_0_), channel_id=1, source_target_pairs={{0,16},{4,20},{8,24},{12,28},{16,0},{20,4},{24,8},{28,12},{1,17},{... | collective-permute-start | bytes 294920 | tf_op jit(solution)/shard_map/ppermute | solution.py:223
  6.6 0.0 collective-permute-start.2
  6.6 1.9 %collective-permute-start.4 = (bf16[2,64,1536]{2,1,0:T(8,128)(2,1)S(1)}, bf16[2,64,1536]{2,1,0:T(8,128)(2,1)S(1)}, u32[]{:S(2)}, u32[]{:S(2)}) collective-permute-start(bf16[2,64,1536]{2,1,0:T(8,128)(2,1)S(1)} %get-tuple-element.32), channel_id=1, source_target_pairs={{0,4},{4,8},{8,12},{12,16},{16,20},{20,24},{24,28},{1,5},{5,9},{9,... | collective-permute-start | bytes 1179656 | tf_op jit(solution)/shard_map/ppermute | solution.py:245
  8.5 0.1 collective-permute-done.refs_1_
  8.5 2.6 %collective-permute-done.1.refs_2_ = bf16[2,16,1536]{2,1,0:T(8,128)(2,1)S(1)} collective-permute-done((bf16[2,16,1536]{2,1,0:T(8,128)(2,1)S(1)}, bf16[2,16,1536]{2,1,0:T(8,128)(2,1)S(1)}, u32[]{:S(2)}, u32[]{:S(2)}) %collective-permute-start.1) | collective-permute-done | bytes 98336 | tf_op jit(solution)/shard_map/ppermute | solution.py:223
  11.1 1.0 %collective-permute-done.2.refs_3_ = bf16[2,16,1536]{2,1,0:T(8,128)(2,1)S(1)} collective-permute-done((bf16[2,16,1536]{2,1,0:T(8,128)(2,1)S(1)}, bf16[2,16,1536]{2,1,0:T(8,128)(2,1)S(1)}, u32[]{:S(2)}, u32[]{:S(2)}) %collective-permute-start.2) | collective-permute-done | bytes 98336 | tf_op jit(solution)/shard_map/ppermute | solution.py:223
  12.2 0.1 collective-permute-start.3
  12.3 2.3 %shard_map.66.refs_3_.turned_ref = bf16[2,1536,768]{2,1,0:T(8,128)(2,1)S(1)} custom-call(bf16[768,1536]{1,0:T(8,128)(2,1)} %mine_hbm.1, bf16[768,1536]{1,0:T(8,128)(2,1)S(1)} %collective-permute-done.5.other_ref, bf16[4,2,16,1536]{3,2,1,0:T(8,128)(2,1)S(1)} %shard_map.65.order_ref.refs_0_.refs_1_), custom_call_target="tpu_custom_call" | custom-call | tf_op jit(solution)/shard_map/pallas_call | solution.py:254
  14.6 0.0 collective-permute-done.4.refs_2_.refs_0_
  14.6 0.0 collective-permute-done.3.refs_1_.refs_2_
  14.6 0.7 %shard_map.68 = bf16[64,1536]{1,0:T(8,128)(2,1)S(1)} custom-call(s32[12,256]{1,0:T(8,128)S(1)} %get-tuple-element.27.width_ref, bf16[128,1536]{1,0:T(8,128)(2,1)S(1)} %get-tuple-element.28.q_ref, bf16[128,1536]{1,0:T(8,128)(2,1)S(1)} %get-tuple-element.29.k_ref, bf16[128,1536]{1,0:T(8,128)(2,1)S(1)} %get-tuple-element.30.v_ref, ...), custom_call_target="tpu_custom_call" | custom-call | flops 1100000000 | bytes 3000000 | tf_op jit(solution)/shard_map/pallas_call | solution.py:264
  15.3 4.0 %collective-permute-start.9 = (bf16[2,32,1536]{2,1,0:T(8,128)(2,1)S(1)}, bf16[2,32,1536]{2,1,0:T(8,128)(2,1)S(1)}, u32[]{:S(2)}, u32[]{:S(2)}) collective-permute-start(bf16[2,32,1536]{2,1,0:T(8,128)(2,1)S(1)} %bitcast.5), channel_id=1, source_target_pairs={{0,16},{4,20},{8,24},{12,28},{16,0},{20,4},{24,8},{28,12},{1,17},{... | collective-permute-start | bytes 589832 | tf_op jit(solution)/shard_map/ppermute | solution.py:223
  19.3 0.7 %shard_map.67 = bf16[64,1536]{1,0:T(8,128)(2,1)S(1)} custom-call(s32[12,256]{1,0:T(8,128)S(1)} %get-tuple-element.27.width_ref, bf16[128,1536]{1,0:T(8,128)(2,1)S(1)} %get-tuple-element.28.q_ref, bf16[128,1536]{1,0:T(8,128)(2,1)S(1)} %get-tuple-element.29.k_ref, bf16[128,1536]{1,0:T(8,128)(2,1)S(1)} %get-tuple-element.30.v_ref, ...), custom_call_target="tpu_custom_call" | custom-call | flops 1100000000 | bytes 3000000 | tf_op jit(solution)/shard_map/pallas_call | solution.py:264
  20.0 0.7 %collective-permute-start.8 = (bf16[2,32,1536]{2,1,0:T(8,128)(2,1)S(1)}, bf16[2,32,1536]{2,1,0:T(8,128)(2,1)S(1)}, u32[]{:S(2)}, u32[]{:S(2)}) collective-permute-start(bf16[2,32,1536]{2,1,0:T(8,128)(2,1)S(1)} %bitcast.2), channel_id=1, source_target_pairs={{0,8},{4,12},{8,0},{12,4},{16,24},{20,28},{24,16},{28,20},{1,9},{5... | collective-permute-start | bytes 589832 | tf_op jit(solution)/shard_map/ppermute | solution.py:223
  20.6 0.8 %shard_map.69 = (bf16[2,2,32,768]{3,2,1,0:T(8,128)(2,1)S(1)}, bf16[2,2,32,768]{3,2,1,0:T(8,128)(2,1)S(1)}) custom-call(bf16[2,32,1536]{2,1,0:T(8,128)(2,1)S(1)} %bitcast.3, bf16[2,32,1536]{2,1,0:T(8,128)(2,1)S(1)} %bitcast.6, bf16[2,1536,768]{2,1,0:T(8,128)(2,1)S(1)} %shard_map.66.refs_3_.turned_ref), custom_call_target="tpu_custom_call" | custom-call | tf_op jit(solution)/shard_map/pallas_call | solution.py:290
  21.4 1.6 %collective-permute-start.6 = (bf16[2,2,32,768]{3,2,1,0:T(8,128)(2,1)S(1)}, bf16[2,2,32,768]{3,2,1,0:T(8,128)(2,1)S(1)}, u32[]{:S(2)}, u32[]{:S(2)}) collective-permute-start(bf16[2,2,32,768]{3,2,1,0:T(8,128)(2,1)S(1)} %get-tuple-element.33), channel_id=1, source_target_pairs={{0,1},{1,0},{2,3},{3,2},{4,5},{5,4},{6,7},{7,6},{8,9},{9,8},{10,11... | collective-permute-start | bytes 589832 | tf_op jit(solution)/shard_map/ppermute | solution.py:221
  23.1 1.4 %collective-permute-start.14 = (bf16[2,32,1536]{2,1,0:T(8,128)(2,1)S(1)}, bf16[2,32,1536]{2,1,0:T(8,128)(2,1)S(1)}, u32[]{:S(2)}, u32[]{:S(2)}) collective-permute-start(bf16[2,32,1536]{2,1,0:T(8,128)(2,1)S(1)} %bitcast.7), channel_id=1, source_target_pairs={{0,8},{4,12},{8,0},{12,4},{16,24},{20,28},{24,16},{28,20},{1,9},{5... | collective-permute-start | bytes 589832 | tf_op jit(solution)/shard_map/ppermute | solution.py:223
  24.5 0.0 collective-permute-start.13
  24.5 2.5 %collective-permute-done.8.high_ref = bf16[2,32,1536]{2,1,0:T(8,128)(2,1)S(1)} collective-permute-done((bf16[2,32,1536]{2,1,0:T(8,128)(2,1)S(1)}, bf16[2,32,1536]{2,1,0:T(8,128)(2,1)S(1)}, u32[]{:S(2)}, u32[]{:S(2)}) %collective-permute-start.8) | collective-permute-done | bytes 196640 | tf_op jit(solution)/shard_map/ppermute | solution.py:223
  27.0 0.8 %shard_map.71 = (bf16[2,2,32,768]{3,2,1,0:T(8,128)(2,1)S(1)}, bf16[2,2,32,768]{3,2,1,0:T(8,128)(2,1)S(1)}) custom-call(bf16[2,32,1536]{2,1,0:T(8,128)(2,1)S(1)} %collective-permute-done.8.high_ref, bf16[2,32,1536]{2,1,0:T(8,128)(2,1)S(1)} %collective-permute-done.9.low_ref, bf16[2,1536,768]{2,1,0:T(8,128)(2,1)S(1)} %shard_map.66.refs_3_.turned_ref, ...), custom_call_target="tpu_custom_call" | custom-call | tf_op jit(solution)/shard_map/pallas_call | solution.py:290
  27.8 1.9 %collective-permute-start.10 = (bf16[2,2,32,768]{3,2,1,0:T(8,128)(2,1)S(1)}, bf16[2,2,32,768]{3,2,1,0:T(8,128)(2,1)S(1)}, u32[]{:S(2)}, u32[]{:S(2)}) collective-permute-start(bf16[2,2,32,768]{3,2,1,0:T(8,128)(2,1)S(1)} %get-tuple-element.37), channel_id=1, source_target_pairs={{0,1},{1,0},{2,3},{3,2},{4,5},{5,4},{6,7},{7,6},{8,9},{9,8},{10,11... | collective-permute-start | bytes 589832 | tf_op jit(solution)/shard_map/ppermute | solution.py:221
  29.7 0.8 %collective-permute-start.19 = (bf16[2,32,1536]{2,1,0:T(8,128)(2,1)S(1)}, bf16[2,32,1536]{2,1,0:T(8,128)(2,1)S(1)}, u32[]{:S(2)}, u32[]{:S(2)}) collective-permute-start(bf16[2,32,1536]{2,1,0:T(8,128)(2,1)S(1)} %collective-permute-done.9.low_ref), channel_id=1, source_target_pairs={{0,8},{4,12},{8,0},{12,4},{16,24},{20,28},{24,16},{28,20},{1,9},{5... | collective-permute-start | bytes 589832 | tf_op jit(solution)/shard_map/ppermute | solution.py:223
  30.5 0.0 collective-permute-done.6.came_ref
  30.5 0.9 %collective-permute-start.18 = (bf16[2,32,1536]{2,1,0:T(8,128)(2,1)S(1)}, bf16[2,32,1536]{2,1,0:T(8,128)(2,1)S(1)}, u32[]{:S(2)}, u32[]{:S(2)}) collective-permute-start(bf16[2,32,1536]{2,1,0:T(8,128)(2,1)S(1)} %collective-permute-done.8.high_ref), channel_id=1, source_target_pairs={{0,16},{4,20},{8,24},{12,28},{16,0},{20,4},{24,8},{28,12},{1,17},{... | collective-permute-start | bytes 589832 | tf_op jit(solution)/shard_map/ppermute | solution.py:223
  31.5 2.6 %collective-permute-start.7 = (bf16[2,32,768]{2,1,0:T(8,128)(2,1)S(1)}, bf16[2,32,768]{2,1,0:T(8,128)(2,1)S(1)}, u32[]{:S(2)}, u32[]{:S(2)}) collective-permute-start(bf16[2,32,768]{2,1,0:T(8,128)(2,1)S(1)} %get-tuple-element.35), channel_id=1, source_target_pairs={{0,2},{1,3},{2,0},{3,1},{4,6},{5,7},{6,4},{7,5},{8,10},{9,11},{10,... | collective-permute-start | bytes 294920 | tf_op jit(solution)/shard_map/ppermute | solution.py:307
  34.1 0.8 %shard_map.73 = (bf16[2,2,32,768]{3,2,1,0:T(8,128)(2,1)S(1)}, bf16[2,2,32,768]{3,2,1,0:T(8,128)(2,1)S(1)}) custom-call(bf16[2,32,1536]{2,1,0:T(8,128)(2,1)S(1)} %collective-permute-done.13.high_ref, bf16[2,32,1536]{2,1,0:T(8,128)(2,1)S(1)} %collective-permute-done.14.low_ref, bf16[2,1536,768]{2,1,0:T(8,128)(2,1)S(1)} %shard_map.66.refs_3_.turned_ref, ...), custom_call_target="tpu_custom_call" | custom-call | tf_op jit(solution)/shard_map/pallas_call | solution.py:290
  34.9 1.2 %collective-permute-start.15 = (bf16[2,2,32,768]{3,2,1,0:T(8,128)(2,1)S(1)}, bf16[2,2,32,768]{3,2,1,0:T(8,128)(2,1)S(1)}, u32[]{:S(2)}, u32[]{:S(2)}) collective-permute-start(bf16[2,2,32,768]{3,2,1,0:T(8,128)(2,1)S(1)} %get-tuple-element.41), channel_id=1, source_target_pairs={{0,1},{1,0},{2,3},{3,2},{4,5},{5,4},{6,7},{7,6},{8,9},{9,8},{10,11... | collective-permute-start | bytes 589832 | tf_op jit(solution)/shard_map/ppermute | solution.py:221
  36.2 1.8 %collective-permute-done.7.refs_2_.refs_0_ = bf16[2,32,768]{2,1,0:T(8,128)(2,1)S(1)} collective-permute-done((bf16[2,32,768]{2,1,0:T(8,128)(2,1)S(1)}, bf16[2,32,768]{2,1,0:T(8,128)(2,1)S(1)}, u32[]{:S(2)}, u32[]{:S(2)}) %collective-permute-start.7) | collective-permute-done | bytes 98336 | tf_op jit(solution)/shard_map/ppermute | solution.py:307
  38.0 0.8 %shard_map.75 = (bf16[2,2,32,768]{3,2,1,0:T(8,128)(2,1)S(1)}, bf16[2,2,32,768]{3,2,1,0:T(8,128)(2,1)S(1)}) custom-call(bf16[2,32,1536]{2,1,0:T(8,128)(2,1)S(1)} %collective-permute-done.18.high_ref, bf16[2,32,1536]{2,1,0:T(8,128)(2,1)S(1)} %collective-permute-done.19.low_ref, bf16[2,1536,768]{2,1,0:T(8,128)(2,1)S(1)} %shard_map.66.refs_3_.turned_ref, ...), custom_call_target="tpu_custom_call" | custom-call | tf_op jit(solution)/shard_map/pallas_call | solution.py:290
  38.8 1.0 %collective-permute-start.20 = (bf16[2,2,32,768]{3,2,1,0:T(8,128)(2,1)S(1)}, bf16[2,2,32,768]{3,2,1,0:T(8,128)(2,1)S(1)}, u32[]{:S(2)}, u32[]{:S(2)}) collective-permute-start(bf16[2,2,32,768]{3,2,1,0:T(8,128)(2,1)S(1)} %get-tuple-element.45), channel_id=1, source_target_pairs={{0,1},{1,0},{2,3},{3,2},{4,5},{5,4},{6,7},{7,6},{8,9},{9,8},{10,11... | collective-permute-start | bytes 589832 | tf_op jit(solution)/shard_map/ppermute | solution.py:221
  39.7 2.6 %collective-permute-start.11 = (bf16[2,32,768]{2,1,0:T(8,128)(2,1)S(1)}, bf16[2,32,768]{2,1,0:T(8,128)(2,1)S(1)}, u32[]{:S(2)}, u32[]{:S(2)}) collective-permute-start(bf16[2,32,768]{2,1,0:T(8,128)(2,1)S(1)} %get-tuple-element.39), channel_id=1, source_target_pairs={{0,10},{1,11},{2,16},{3,17},{4,14},{5,15},{6,20},{7,21},{8,2},{9,3... | collective-permute-start | bytes 294920 | tf_op jit(solution)/shard_map/ppermute | solution.py:307
  42.3 2.6 %collective-permute-start.12 = (bf16[2,32,768]{2,1,0:T(8,128)(2,1)S(1)}, bf16[2,32,768]{2,1,0:T(8,128)(2,1)S(1)}, u32[]{:S(2)}, u32[]{:S(2)}) collective-permute-start(bf16[2,32,768]{2,1,0:T(8,128)(2,1)S(1)} %get-tuple-element.40.refs_1_), channel_id=1, source_target_pairs={{0,16},{1,17},{2,10},{3,11},{4,20},{5,21},{6,14},{7,15},{8,24},{9,... | collective-permute-start | bytes 294920 | tf_op jit(solution)/shard_map/ppermute | solution.py:307
  44.9 0.0 collective-permute-done.15.came_ref
  44.9 0.1 collective-permute-start.16
  45.0 1.5 %collective-permute-start.17 = (bf16[2,32,768]{2,1,0:T(8,128)(2,1)S(1)}, bf16[2,32,768]{2,1,0:T(8,128)(2,1)S(1)}, u32[]{:S(2)}, u32[]{:S(2)}) collective-permute-start(bf16[2,32,768]{2,1,0:T(8,128)(2,1)S(1)} %get-tuple-element.44), channel_id=1, source_target_pairs={{0,8},{1,9},{2,18},{3,19},{4,12},{5,13},{6,22},{7,23},{8,0},{9,1},... | collective-permute-start | bytes 294920 | tf_op jit(solution)/shard_map/ppermute | solution.py:307
  46.5 0.0 collective-permute-done.11.refs_0_.refs_2_
  46.5 0.0 collective-permute-done.20.came_ref
  46.6 4.6 %collective-permute-start.21 = (bf16[2,32,768]{2,1,0:T(8,128)(2,1)S(1)}, bf16[2,32,768]{2,1,0:T(8,128)(2,1)S(1)}, u32[]{:S(2)}, u32[]{:S(2)}) collective-permute-start(bf16[2,32,768]{2,1,0:T(8,128)(2,1)S(1)} %get-tuple-element.47), channel_id=1, source_target_pairs={{0,26},{1,27},{2,24},{3,25},{4,30},{5,31},{6,28},{7,29},{8,18},{9,... | collective-permute-start | bytes 294920 | tf_op jit(solution)/shard_map/ppermute | solution.py:307
  51.1 2.1 %collective-permute-start.22 = (bf16[2,32,768]{2,1,0:T(8,128)(2,1)S(1)}, bf16[2,32,768]{2,1,0:T(8,128)(2,1)S(1)}, u32[]{:S(2)}, u32[]{:S(2)}) collective-permute-start(bf16[2,32,768]{2,1,0:T(8,128)(2,1)S(1)} %get-tuple-element.48), channel_id=1, source_target_pairs={{0,24},{1,25},{2,26},{3,27},{4,28},{5,29},{6,30},{7,31},{8,16},{9,... | collective-permute-start | bytes 294920 | tf_op jit(solution)/shard_map/ppermute | solution.py:307
  53.2 0.0 collective-permute-done.16.refs_4_
  53.2 0.0 collective-permute-done.17.refs_5_
  53.2 0.0 collective-permute-done.12.refs_3_
  53.2 0.7 %collective-permute-done.21.refs_6_ = bf16[2,32,768]{2,1,0:T(8,128)(2,1)S(1)} collective-permute-done((bf16[2,32,768]{2,1,0:T(8,128)(2,1)S(1)}, bf16[2,32,768]{2,1,0:T(8,128)(2,1)S(1)}, u32[]{:S(2)}, u32[]{:S(2)}) %collective-permute-start.21) | collective-permute-done | bytes 98336 | tf_op jit(solution)/shard_map/ppermute | solution.py:307
  53.9 2.7 %collective-permute-done.22.refs_7_ = bf16[2,32,768]{2,1,0:T(8,128)(2,1)S(1)} collective-permute-done((bf16[2,32,768]{2,1,0:T(8,128)(2,1)S(1)}, bf16[2,32,768]{2,1,0:T(8,128)(2,1)S(1)}, u32[]{:S(2)}, u32[]{:S(2)}) %collective-permute-start.22) | collective-permute-done | bytes 98336 | tf_op jit(solution)/shard_map/ppermute | solution.py:307
  56.6 0.8 %shard_map.77 = bf16[32,6144]{1,0:T(8,128)(2,1)} custom-call(bf16[2,32,768]{2,1,0:T(8,128)(2,1)S(1)} %collective-permute-done.7.refs_2_.refs_0_, bf16[2,32,768]{2,1,0:T(8,128)(2,1)S(1)} %get-tuple-element.36.refs_1_, bf16[2,32,768]{2,1,0:T(8,128)(2,1)S(1)} %collective-permute-done.11.refs_0_.refs_2_, ...), custom_call_target="tpu_custom_call" | custom-call | tf_op jit(solution)/shard_map/pallas_call | solution.py:323
  (12 shorter events, 0.2 us)
Async XLA Ops:
  0.0 12.2 %collective-permute-start.5 = (bf16[768,1536]{1,0:T(8,128)(2,1)}, bf16[768,1536]{1,0:T(8,128)(2,1)S(1)}, u32[]{:S(2)}, u32[]{:S(2)}) collective-permute-start(bf16[768,1536]{1,0:T(8,128)(2,1)} %mine_hbm.1), channel_id=1, source_target_pairs={{0,4},{4,0},{8,12},{12,8},{16,20},{20,16},{24,28},{28,24},{1,5},{5... | collective-permute-start | bytes 7077896 | tf_op jit(solution)/shard_map/ppermute | solution.py:223
  2.5 6.0 %collective-permute-start = (bf16[2,16,1536]{2,1,0:T(8,128)(2,1)S(1)}, bf16[2,16,1536]{2,1,0:T(8,128)(2,1)S(1)}, u32[]{:S(2)}, u32[]{:S(2)}) collective-permute-start(bf16[2,16,1536]{2,1,0:T(8,128)(2,1)S(1)} %get-tuple-element.31.refs_0_), channel_id=1, source_target_pairs={{0,8},{4,12},{8,0},{12,4},{16,24},{20,28},{24,16},{28,20},{1,9},{5... | collective-permute-start | bytes 294920 | tf_op jit(solution)/shard_map/ppermute | solution.py:223
  5.1 6.1 %collective-permute-start.1 = (bf16[2,16,1536]{2,1,0:T(8,128)(2,1)S(1)}, bf16[2,16,1536]{2,1,0:T(8,128)(2,1)S(1)}, u32[]{:S(2)}, u32[]{:S(2)}) collective-permute-start(bf16[2,16,1536]{2,1,0:T(8,128)(2,1)S(1)} %get-tuple-element.31.refs_0_), channel_id=1, source_target_pairs={{0,16},{4,20},{8,24},{12,28},{16,0},{20,4},{24,8},{28,12},{1,17},{... | collective-permute-start | bytes 294920 | tf_op jit(solution)/shard_map/ppermute | solution.py:223
  6.6 5.5 %collective-permute-start.2 = (bf16[2,16,1536]{2,1,0:T(8,128)(2,1)S(1)}, bf16[2,16,1536]{2,1,0:T(8,128)(2,1)S(1)}, u32[]{:S(2)}, u32[]{:S(2)}) collective-permute-start(bf16[2,16,1536]{2,1,0:T(8,128)(2,1)S(1)} %get-tuple-element.31.refs_0_), channel_id=1, source_target_pairs={{0,24},{4,28},{8,16},{12,20},{16,8},{20,12},{24,0},{28,4},{1,25},{... | collective-permute-start | bytes 294920 | tf_op jit(solution)/shard_map/ppermute | solution.py:223
  6.6 8.0 %collective-permute-start.4 = (bf16[2,64,1536]{2,1,0:T(8,128)(2,1)S(1)}, bf16[2,64,1536]{2,1,0:T(8,128)(2,1)S(1)}, u32[]{:S(2)}, u32[]{:S(2)}) collective-permute-start(bf16[2,64,1536]{2,1,0:T(8,128)(2,1)S(1)} %get-tuple-element.32), channel_id=1, source_target_pairs={{0,4},{4,8},{8,12},{12,16},{16,20},{20,24},{24,28},{1,5},{5,9},{9,... | collective-permute-start | bytes 1179656 | tf_op jit(solution)/shard_map/ppermute | solution.py:245
  12.2 2.5 %collective-permute-start.3 = (bf16[4,2,16,1536]{3,2,1,0:T(8,128)(2,1)S(1)}, bf16[4,2,16,1536]{3,2,1,0:T(8,128)(2,1)S(1)}, u32[]{:S(2)}, u32[]{:S(2)}) collective-permute-start(bf16[4,2,16,1536]{3,2,1,0:T(8,128)(2,1)S(1)} %shard_map.65.order_ref.refs_0_.refs_1_), channel_id=1, source_target_pairs={{0,4},{4,0},{8,12},{12,8},{16,20},{20,16},{24,28},{28,24},{1,5},{5... | collective-permute-start | bytes 1179656 | tf_op jit(solution)/shard_map/ppermute | solution.py:223
  15.3 9.2 %collective-permute-start.9 = (bf16[2,32,1536]{2,1,0:T(8,128)(2,1)S(1)}, bf16[2,32,1536]{2,1,0:T(8,128)(2,1)S(1)}, u32[]{:S(2)}, u32[]{:S(2)}) collective-permute-start(bf16[2,32,1536]{2,1,0:T(8,128)(2,1)S(1)} %bitcast.5), channel_id=1, source_target_pairs={{0,16},{4,20},{8,24},{12,28},{16,0},{20,4},{24,8},{28,12},{1,17},{... | collective-permute-start | bytes 589832 | tf_op jit(solution)/shard_map/ppermute | solution.py:223
  20.0 7.0 %collective-permute-start.8 = (bf16[2,32,1536]{2,1,0:T(8,128)(2,1)S(1)}, bf16[2,32,1536]{2,1,0:T(8,128)(2,1)S(1)}, u32[]{:S(2)}, u32[]{:S(2)}) collective-permute-start(bf16[2,32,1536]{2,1,0:T(8,128)(2,1)S(1)} %bitcast.2), channel_id=1, source_target_pairs={{0,8},{4,12},{8,0},{12,4},{16,24},{20,28},{24,16},{28,20},{1,9},{5... | collective-permute-start | bytes 589832 | tf_op jit(solution)/shard_map/ppermute | solution.py:223
  21.4 9.1 %collective-permute-start.6 = (bf16[2,2,32,768]{3,2,1,0:T(8,128)(2,1)S(1)}, bf16[2,2,32,768]{3,2,1,0:T(8,128)(2,1)S(1)}, u32[]{:S(2)}, u32[]{:S(2)}) collective-permute-start(bf16[2,2,32,768]{3,2,1,0:T(8,128)(2,1)S(1)} %get-tuple-element.33), channel_id=1, source_target_pairs={{0,1},{1,0},{2,3},{3,2},{4,5},{5,4},{6,7},{7,6},{8,9},{9,8},{10,11... | collective-permute-start | bytes 589832 | tf_op jit(solution)/shard_map/ppermute | solution.py:221
  23.1 8.4 %collective-permute-start.14 = (bf16[2,32,1536]{2,1,0:T(8,128)(2,1)S(1)}, bf16[2,32,1536]{2,1,0:T(8,128)(2,1)S(1)}, u32[]{:S(2)}, u32[]{:S(2)}) collective-permute-start(bf16[2,32,1536]{2,1,0:T(8,128)(2,1)S(1)} %bitcast.7), channel_id=1, source_target_pairs={{0,8},{4,12},{8,0},{12,4},{16,24},{20,28},{24,16},{28,20},{1,9},{5... | collective-permute-start | bytes 589832 | tf_op jit(solution)/shard_map/ppermute | solution.py:223
  24.5 9.6 %collective-permute-start.13 = (bf16[2,32,1536]{2,1,0:T(8,128)(2,1)S(1)}, bf16[2,32,1536]{2,1,0:T(8,128)(2,1)S(1)}, u32[]{:S(2)}, u32[]{:S(2)}) collective-permute-start(bf16[2,32,1536]{2,1,0:T(8,128)(2,1)S(1)} %bitcast.4), channel_id=1, source_target_pairs={{0,16},{4,20},{8,24},{12,28},{16,0},{20,4},{24,8},{28,12},{1,17},{... | collective-permute-start | bytes 589832 | tf_op jit(solution)/shard_map/ppermute | solution.py:223
  27.8 8.3 %collective-permute-start.10 = (bf16[2,2,32,768]{3,2,1,0:T(8,128)(2,1)S(1)}, bf16[2,2,32,768]{3,2,1,0:T(8,128)(2,1)S(1)}, u32[]{:S(2)}, u32[]{:S(2)}) collective-permute-start(bf16[2,2,32,768]{3,2,1,0:T(8,128)(2,1)S(1)} %get-tuple-element.37), channel_id=1, source_target_pairs={{0,1},{1,0},{2,3},{3,2},{4,5},{5,4},{6,7},{7,6},{8,9},{9,8},{10,11... | collective-permute-start | bytes 589832 | tf_op jit(solution)/shard_map/ppermute | solution.py:221
  29.7 8.2 %collective-permute-start.19 = (bf16[2,32,1536]{2,1,0:T(8,128)(2,1)S(1)}, bf16[2,32,1536]{2,1,0:T(8,128)(2,1)S(1)}, u32[]{:S(2)}, u32[]{:S(2)}) collective-permute-start(bf16[2,32,1536]{2,1,0:T(8,128)(2,1)S(1)} %collective-permute-done.9.low_ref), channel_id=1, source_target_pairs={{0,8},{4,12},{8,0},{12,4},{16,24},{20,28},{24,16},{28,20},{1,9},{5... | collective-permute-start | bytes 589832 | tf_op jit(solution)/shard_map/ppermute | solution.py:223
  30.5 7.4 %collective-permute-start.18 = (bf16[2,32,1536]{2,1,0:T(8,128)(2,1)S(1)}, bf16[2,32,1536]{2,1,0:T(8,128)(2,1)S(1)}, u32[]{:S(2)}, u32[]{:S(2)}) collective-permute-start(bf16[2,32,1536]{2,1,0:T(8,128)(2,1)S(1)} %collective-permute-done.8.high_ref), channel_id=1, source_target_pairs={{0,16},{4,20},{8,24},{12,28},{16,0},{20,4},{24,8},{28,12},{1,17},{... | collective-permute-start | bytes 589832 | tf_op jit(solution)/shard_map/ppermute | solution.py:223
  31.5 6.5 %collective-permute-start.7 = (bf16[2,32,768]{2,1,0:T(8,128)(2,1)S(1)}, bf16[2,32,768]{2,1,0:T(8,128)(2,1)S(1)}, u32[]{:S(2)}, u32[]{:S(2)}) collective-permute-start(bf16[2,32,768]{2,1,0:T(8,128)(2,1)S(1)} %get-tuple-element.35), channel_id=1, source_target_pairs={{0,2},{1,3},{2,0},{3,1},{4,6},{5,7},{6,4},{7,5},{8,10},{9,11},{10,... | collective-permute-start | bytes 294920 | tf_op jit(solution)/shard_map/ppermute | solution.py:307
  34.9 10.0 %collective-permute-start.15 = (bf16[2,2,32,768]{3,2,1,0:T(8,128)(2,1)S(1)}, bf16[2,2,32,768]{3,2,1,0:T(8,128)(2,1)S(1)}, u32[]{:S(2)}, u32[]{:S(2)}) collective-permute-start(bf16[2,2,32,768]{3,2,1,0:T(8,128)(2,1)S(1)} %get-tuple-element.41), channel_id=1, source_target_pairs={{0,1},{1,0},{2,3},{3,2},{4,5},{5,4},{6,7},{7,6},{8,9},{9,8},{10,11... | collective-permute-start | bytes 589832 | tf_op jit(solution)/shard_map/ppermute | solution.py:221
  38.8 7.8 %collective-permute-start.20 = (bf16[2,2,32,768]{3,2,1,0:T(8,128)(2,1)S(1)}, bf16[2,2,32,768]{3,2,1,0:T(8,128)(2,1)S(1)}, u32[]{:S(2)}, u32[]{:S(2)}) collective-permute-start(bf16[2,2,32,768]{3,2,1,0:T(8,128)(2,1)S(1)} %get-tuple-element.45), channel_id=1, source_target_pairs={{0,1},{1,0},{2,3},{3,2},{4,5},{5,4},{6,7},{7,6},{8,9},{9,8},{10,11... | collective-permute-start | bytes 589832 | tf_op jit(solution)/shard_map/ppermute | solution.py:221
  39.7 6.8 %collective-permute-start.11 = (bf16[2,32,768]{2,1,0:T(8,128)(2,1)S(1)}, bf16[2,32,768]{2,1,0:T(8,128)(2,1)S(1)}, u32[]{:S(2)}, u32[]{:S(2)}) collective-permute-start(bf16[2,32,768]{2,1,0:T(8,128)(2,1)S(1)} %get-tuple-element.39), channel_id=1, source_target_pairs={{0,10},{1,11},{2,16},{3,17},{4,14},{5,15},{6,20},{7,21},{8,2},{9,3... | collective-permute-start | bytes 294920 | tf_op jit(solution)/shard_map/ppermute | solution.py:307
  42.3 10.9 %collective-permute-start.12 = (bf16[2,32,768]{2,1,0:T(8,128)(2,1)S(1)}, bf16[2,32,768]{2,1,0:T(8,128)(2,1)S(1)}, u32[]{:S(2)}, u32[]{:S(2)}) collective-permute-start(bf16[2,32,768]{2,1,0:T(8,128)(2,1)S(1)} %get-tuple-element.40.refs_1_), channel_id=1, source_target_pairs={{0,16},{1,17},{2,10},{3,11},{4,20},{5,21},{6,14},{7,15},{8,24},{9,... | collective-permute-start | bytes 294920 | tf_op jit(solution)/shard_map/ppermute | solution.py:307
  44.9 8.3 %collective-permute-start.16 = (bf16[2,32,768]{2,1,0:T(8,128)(2,1)S(1)}, bf16[2,32,768]{2,1,0:T(8,128)(2,1)S(1)}, u32[]{:S(2)}, u32[]{:S(2)}) collective-permute-start(bf16[2,32,768]{2,1,0:T(8,128)(2,1)S(1)} %get-tuple-element.43), channel_id=1, source_target_pairs={{0,18},{1,19},{2,8},{3,9},{4,22},{5,23},{6,12},{7,13},{8,26},{9,27... | collective-permute-start | bytes 294920 | tf_op jit(solution)/shard_map/ppermute | solution.py:307
  45.0 8.2 %collective-permute-start.17 = (bf16[2,32,768]{2,1,0:T(8,128)(2,1)S(1)}, bf16[2,32,768]{2,1,0:T(8,128)(2,1)S(1)}, u32[]{:S(2)}, u32[]{:S(2)}) collective-permute-start(bf16[2,32,768]{2,1,0:T(8,128)(2,1)S(1)} %get-tuple-element.44), channel_id=1, source_target_pairs={{0,8},{1,9},{2,18},{3,19},{4,12},{5,13},{6,22},{7,23},{8,0},{9,1},... | collective-permute-start | bytes 294920 | tf_op jit(solution)/shard_map/ppermute | solution.py:307
  46.6 7.4 %collective-permute-start.21 = (bf16[2,32,768]{2,1,0:T(8,128)(2,1)S(1)}, bf16[2,32,768]{2,1,0:T(8,128)(2,1)S(1)}, u32[]{:S(2)}, u32[]{:S(2)}) collective-permute-start(bf16[2,32,768]{2,1,0:T(8,128)(2,1)S(1)} %get-tuple-element.47), channel_id=1, source_target_pairs={{0,26},{1,27},{2,24},{3,25},{4,30},{5,31},{6,28},{7,29},{8,18},{9,... | collective-permute-start | bytes 294920 | tf_op jit(solution)/shard_map/ppermute | solution.py:307
  51.1 5.5 %collective-permute-start.22 = (bf16[2,32,768]{2,1,0:T(8,128)(2,1)S(1)}, bf16[2,32,768]{2,1,0:T(8,128)(2,1)S(1)}, u32[]{:S(2)}, u32[]{:S(2)}) collective-permute-start(bf16[2,32,768]{2,1,0:T(8,128)(2,1)S(1)} %get-tuple-element.48), channel_id=1, source_target_pairs={{0,24},{1,25},{2,26},{3,27},{4,28},{5,29},{6,30},{7,31},{8,16},{9,... | collective-permute-start | bytes 294920 | tf_op jit(solution)/shard_map/ppermute | solution.py:307

commit v3 on v2

--- a/solution.py
+++ b/solution.py
@@ -176,6 +176,10 @@
     for ref, which in ((away_ref, side), (stay_ref, 1 - side)):
         total = came_ref[:, which].astype(jnp.float32) + keep_ref[:, which].astype(jnp.float32)
         ref[...] = total.astype(BF16)
+
+
+def hand_on_kernel(stay_ref, order_ref, out_ref):
+    out_ref[...] = stay_ref[...]
 
 
 def join_kernel(chunks, *refs):
@@ -318,7 +322,18 @@
             out_specs=(vmem(),) * 2,
             compiler_params=PARAMS,
         )(came, keeps[n], *arrays)
-        found[n] = (owned(aways[n], high, low, True), owned(stays[n], high, low, False))
+        found[n] = [owned(aways[n], high, low, True), None]
+        if n != 1:
+            found[n][1] = owned(stays[n], high, low, False)
+        if n == min(2, chips - 1) and chips > 1:
+            stay = pl.pallas_call(
+                hand_on_kernel,
+                out_shape=shaped(2, rows, wide),
+                in_specs=[vmem(), pl.BlockSpec(memory_space=pl.ANY)],
+                out_specs=vmem(),
+                compiler_params=PARAMS,
+            )(stays[1], aways[n])
+            found[1][1] = owned(stay, *chunks[1], False)
     flat = wide % 128 == 0
     joined = pl.pallas_call(
         functools.partial(join_kernel, chunks),

time: 58.1 us -> 58.1 us (level)
  transfers between devices with their start and end apart: 23 -> 23, of which waited for: 7 -> 8; matrix products, arithmetic and copies ran while one was open for 0% -> 0% of each run, Pallas kernels for 15% -> 15%
where the time goes in v3:
time: 58.1 us; the launch traced here: 57.6 us
  starting transfers between devices  35.9 us (62%)
  waiting for transfers between devices  11.6 us (20%)
  Pallas kernels  9.9 us (17%)
    ppermute x7, starting transfers between devices, owned(): return lax.ppermute(value, ('seq', 'head'), pairs)  15.9 us
    ppermute x11, starting transfers between devices, swap(): return lax.ppermute(value, 'seq', [(i, i ^ k) for i in range(seq)])  12.4 us
    ppermute x11, waiting for transfers between devices, swap(): return lax.ppermute(value, 'seq', [(i, i ^ k) for i in range(seq)])  6.16 us
    ppermute x4, starting transfers between devices, swap(): return lax.ppermute(value, 'head', [(i, i ^ z) for i in range(groups)])  5.78 us
    ppermute x7, waiting for transfers between devices, owned(): return lax.ppermute(value, ('seq', 'head'), pairs)  5.29 us
    pallas_call x4, Pallas kernels, projected(): pl.pallas_call(project_kernel, out_shape=(shaped(2, half, rows, wide),) *...  3.13 us
    pallas_call x1, Pallas kernels, local(): pl.pallas_call(turn_kernel, out_shape=shaped(2, feat, wide), in_specs=[hb...  2.35 us
    pallas_call x1, Pallas kernels, local(): pl.pallas_call(pick_kernel, out_shape=(shaped(2, per_block, feat), shaped...  2.05 us
  transfers between devices with their start and end apart: 23, of which 8 were waited for; matrix products, arithmetic and copies ran while one was open for 0% of the time, Pallas kernels for 15%

profile of v3, /device:TPU:0, one launch (start us, length us, event | category | flops | bytes accessed | tf_op | source)
XLA Modules:
  0.0 57.6 jit_solution(3242900767896963415)
XLA Ops:
  0.0 0.5 collective-permute-start.5
  0.5 2.1 %shard_map.64 = (bf16[2,16,1536]{2,1,0:T(8,128)(2,1)S(1)}, bf16[2,64,1536]{2,1,0:T(8,128)(2,1)S(1)}, s32[12,256]{1,0:T(8,128)S(1)}, bf16[128,1536]{1,0:T(8,128)(...) custom-call(s32[1,16]{1,0:T(1,128)} %picks_ref.1, s32[12]{0:T(128)} %band_ref.1, ...), custom_call_target="tpu_custom_call" | custom-call | tf_op jit(solution)/shard_map/pallas_call | solution.py:235
  2.5 2.6 %collective-permute-start = (bf16[2,16,1536]{2,1,0:T(8,128)(2,1)S(1)}, bf16[2,16,1536]{2,1,0:T(8,128)(2,1)S(1)}, u32[]{:S(2)}, u32[]{:S(2)}) collective-permute-start(bf16[2,16,1536]{2,1,0:T(8,128)(2,1)S(1)} %get-tuple-element.31.refs_0_), channel_id=1, source_target_pairs={{0,8},{4,12},{8,0},{12,4},{16,24},{20,28},{24,16},{28,20},{1,9},{5... | collective-permute-start | bytes 294920 | tf_op jit(solution)/shard_map/ppermute | solution.py:227
  5.1 1.5 %collective-permute-start.1 = (bf16[2,16,1536]{2,1,0:T(8,128)(2,1)S(1)}, bf16[2,16,1536]{2,1,0:T(8,128)(2,1)S(1)}, u32[]{:S(2)}, u32[]{:S(2)}) collective-permute-start(bf16[2,16,1536]{2,1,0:T(8,128)(2,1)S(1)} %get-tuple-element.31.refs_0_), channel_id=1, source_target_pairs={{0,16},{4,20},{8,24},{12,28},{16,0},{20,4},{24,8},{28,12},{1,17},{... | collective-permute-start | bytes 294920 | tf_op jit(solution)/shard_map/ppermute | solution.py:227
  6.6 0.0 collective-permute-start.2
  6.6 1.9 %collective-permute-start.4 = (bf16[2,64,1536]{2,1,0:T(8,128)(2,1)S(1)}, bf16[2,64,1536]{2,1,0:T(8,128)(2,1)S(1)}, u32[]{:S(2)}, u32[]{:S(2)}) collective-permute-start(bf16[2,64,1536]{2,1,0:T(8,128)(2,1)S(1)} %get-tuple-element.32), channel_id=1, source_target_pairs={{0,4},{4,8},{8,12},{12,16},{16,20},{20,24},{24,28},{1,5},{5,9},{9,... | collective-permute-start | bytes 1179656 | tf_op jit(solution)/shard_map/ppermute | solution.py:249
  8.5 0.1 collective-permute-done.refs_1_
  8.5 2.6 %collective-permute-done.1.refs_2_ = bf16[2,16,1536]{2,1,0:T(8,128)(2,1)S(1)} collective-permute-done((bf16[2,16,1536]{2,1,0:T(8,128)(2,1)S(1)}, bf16[2,16,1536]{2,1,0:T(8,128)(2,1)S(1)}, u32[]{:S(2)}, u32[]{:S(2)}) %collective-permute-start.1) | collective-permute-done | bytes 98336 | tf_op jit(solution)/shard_map/ppermute | solution.py:227
  11.1 1.0 %collective-permute-done.2.refs_3_ = bf16[2,16,1536]{2,1,0:T(8,128)(2,1)S(1)} collective-permute-done((bf16[2,16,1536]{2,1,0:T(8,128)(2,1)S(1)}, bf16[2,16,1536]{2,1,0:T(8,128)(2,1)S(1)}, u32[]{:S(2)}, u32[]{:S(2)}) %collective-permute-start.2) | collective-permute-done | bytes 98336 | tf_op jit(solution)/shard_map/ppermute | solution.py:227
  12.2 0.1 collective-permute-start.3
  12.2 0.0 collective-permute-done.5.other_ref
  12.3 2.3 %shard_map.66.refs_3_.turned_ref = bf16[2,1536,768]{2,1,0:T(8,128)(2,1)S(1)} custom-call(bf16[768,1536]{1,0:T(8,128)(2,1)} %mine_hbm.1, bf16[768,1536]{1,0:T(8,128)(2,1)S(1)} %collective-permute-done.5.other_ref, bf16[4,2,16,1536]{3,2,1,0:T(8,128)(2,1)S(1)} %shard_map.65.order_ref.refs_0_.refs_1_), custom_call_target="tpu_custom_call" | custom-call | tf_op jit(solution)/shard_map/pallas_call | solution.py:258
  14.6 0.0 collective-permute-done.4.refs_2_.refs_0_
  14.6 0.0 collective-permute-done.3.refs_1_.refs_2_
  14.6 0.7 %shard_map.68 = bf16[64,1536]{1,0:T(8,128)(2,1)S(1)} custom-call(s32[12,256]{1,0:T(8,128)S(1)} %get-tuple-element.27.width_ref, bf16[128,1536]{1,0:T(8,128)(2,1)S(1)} %get-tuple-element.28.q_ref, bf16[128,1536]{1,0:T(8,128)(2,1)S(1)} %get-tuple-element.29.k_ref, bf16[128,1536]{1,0:T(8,128)(2,1)S(1)} %get-tuple-element.30.v_ref, ...), custom_call_target="tpu_custom_call" | custom-call | flops 1100000000 | bytes 3000000 | tf_op jit(solution)/shard_map/pallas_call | solution.py:268
  15.3 4.0 %collective-permute-start.9 = (bf16[2,32,1536]{2,1,0:T(8,128)(2,1)S(1)}, bf16[2,32,1536]{2,1,0:T(8,128)(2,1)S(1)}, u32[]{:S(2)}, u32[]{:S(2)}) collective-permute-start(bf16[2,32,1536]{2,1,0:T(8,128)(2,1)S(1)} %bitcast.5), channel_id=1, source_target_pairs={{0,16},{4,20},{8,24},{12,28},{16,0},{20,4},{24,8},{28,12},{1,17},{... | collective-permute-start | bytes 589832 | tf_op jit(solution)/shard_map/ppermute | solution.py:227
  19.3 0.7 %shard_map.67 = bf16[64,1536]{1,0:T(8,128)(2,1)S(1)} custom-call(s32[12,256]{1,0:T(8,128)S(1)} %get-tuple-element.27.width_ref, bf16[128,1536]{1,0:T(8,128)(2,1)S(1)} %get-tuple-element.28.q_ref, bf16[128,1536]{1,0:T(8,128)(2,1)S(1)} %get-tuple-element.29.k_ref, bf16[128,1536]{1,0:T(8,128)(2,1)S(1)} %get-tuple-element.30.v_ref, ...), custom_call_target="tpu_custom_call" | custom-call | flops 1100000000 | bytes 3000000 | tf_op jit(solution)/shard_map/pallas_call | solution.py:268
  20.0 0.7 %collective-permute-start.8 = (bf16[2,32,1536]{2,1,0:T(8,128)(2,1)S(1)}, bf16[2,32,1536]{2,1,0:T(8,128)(2,1)S(1)}, u32[]{:S(2)}, u32[]{:S(2)}) collective-permute-start(bf16[2,32,1536]{2,1,0:T(8,128)(2,1)S(1)} %bitcast.2), channel_id=1, source_target_pairs={{0,8},{4,12},{8,0},{12,4},{16,24},{20,28},{24,16},{28,20},{1,9},{5... | collective-permute-start | bytes 589832 | tf_op jit(solution)/shard_map/ppermute | solution.py:227
  20.6 0.8 %shard_map.69 = (bf16[2,2,32,768]{3,2,1,0:T(8,128)(2,1)S(1)}, bf16[2,2,32,768]{3,2,1,0:T(8,128)(2,1)S(1)}) custom-call(bf16[2,32,1536]{2,1,0:T(8,128)(2,1)S(1)} %bitcast.3, bf16[2,32,1536]{2,1,0:T(8,128)(2,1)S(1)} %bitcast.6, bf16[2,1536,768]{2,1,0:T(8,128)(2,1)S(1)} %shard_map.66.refs_3_.turned_ref), custom_call_target="tpu_custom_call" | custom-call | tf_op jit(solution)/shard_map/pallas_call | solution.py:294
  21.4 1.6 %collective-permute-start.6 = (bf16[2,2,32,768]{3,2,1,0:T(8,128)(2,1)S(1)}, bf16[2,2,32,768]{3,2,1,0:T(8,128)(2,1)S(1)}, u32[]{:S(2)}, u32[]{:S(2)}) collective-permute-start(bf16[2,2,32,768]{3,2,1,0:T(8,128)(2,1)S(1)} %get-tuple-element.33), channel_id=1, source_target_pairs={{0,1},{1,0},{2,3},{3,2},{4,5},{5,4},{6,7},{7,6},{8,9},{9,8},{10,11... | collective-permute-start | bytes 589832 | tf_op jit(solution)/shard_map/ppermute | solution.py:225
  23.1 1.4 %collective-permute-start.13 = (bf16[2,32,1536]{2,1,0:T(8,128)(2,1)S(1)}, bf16[2,32,1536]{2,1,0:T(8,128)(2,1)S(1)}, u32[]{:S(2)}, u32[]{:S(2)}) collective-permute-start(bf16[2,32,1536]{2,1,0:T(8,128)(2,1)S(1)} %bitcast.7), channel_id=1, source_target_pairs={{0,8},{4,12},{8,0},{12,4},{16,24},{20,28},{24,16},{28,20},{1,9},{5... | collective-permute-start | bytes 589832 | tf_op jit(solution)/shard_map/ppermute | solution.py:227
  24.5 0.0 collective-permute-start.12
  24.5 0.0 collective-permute-done.9.low_ref
  24.5 2.5 %collective-permute-done.8.high_ref = bf16[2,32,1536]{2,1,0:T(8,128)(2,1)S(1)} collective-permute-done((bf16[2,32,1536]{2,1,0:T(8,128)(2,1)S(1)}, bf16[2,32,1536]{2,1,0:T(8,128)(2,1)S(1)}, u32[]{:S(2)}, u32[]{:S(2)}) %collective-permute-start.8) | collective-permute-done | bytes 196640 | tf_op jit(solution)/shard_map/ppermute | solution.py:227
  27.0 0.8 %shard_map.71 = (bf16[2,2,32,768]{3,2,1,0:T(8,128)(2,1)S(1)}, bf16[2,2,32,768]{3,2,1,0:T(8,128)(2,1)S(1)}) custom-call(bf16[2,32,1536]{2,1,0:T(8,128)(2,1)S(1)} %collective-permute-done.8.high_ref, bf16[2,32,1536]{2,1,0:T(8,128)(2,1)S(1)} %collective-permute-done.9.low_ref, bf16[2,1536,768]{2,1,0:T(8,128)(2,1)S(1)} %shard_map.66.refs_3_.turned_ref, ...), custom_call_target="tpu_custom_call" | custom-call | tf_op jit(solution)/shard_map/pallas_call | solution.py:294
  27.8 1.9 %collective-permute-start.10 = (bf16[2,2,32,768]{3,2,1,0:T(8,128)(2,1)S(1)}, bf16[2,2,32,768]{3,2,1,0:T(8,128)(2,1)S(1)}, u32[]{:S(2)}, u32[]{:S(2)}) collective-permute-start(bf16[2,2,32,768]{3,2,1,0:T(8,128)(2,1)S(1)} %get-tuple-element.37), channel_id=1, source_target_pairs={{0,1},{1,0},{2,3},{3,2},{4,5},{5,4},{6,7},{7,6},{8,9},{9,8},{10,11... | collective-permute-start | bytes 589832 | tf_op jit(solution)/shard_map/ppermute | solution.py:225
  29.7 0.8 %collective-permute-start.19 = (bf16[2,32,1536]{2,1,0:T(8,128)(2,1)S(1)}, bf16[2,32,1536]{2,1,0:T(8,128)(2,1)S(1)}, u32[]{:S(2)}, u32[]{:S(2)}) collective-permute-start(bf16[2,32,1536]{2,1,0:T(8,128)(2,1)S(1)} %collective-permute-done.9.low_ref), channel_id=1, source_target_pairs={{0,8},{4,12},{8,0},{12,4},{16,24},{20,28},{24,16},{28,20},{1,9},{5... | collective-permute-start | bytes 589832 | tf_op jit(solution)/shard_map/ppermute | solution.py:227
  30.5 0.9 %collective-permute-start.18 = (bf16[2,32,1536]{2,1,0:T(8,128)(2,1)S(1)}, bf16[2,32,1536]{2,1,0:T(8,128)(2,1)S(1)}, u32[]{:S(2)}, u32[]{:S(2)}) collective-permute-start(bf16[2,32,1536]{2,1,0:T(8,128)(2,1)S(1)} %collective-permute-done.8.high_ref), channel_id=1, source_target_pairs={{0,16},{4,20},{8,24},{12,28},{16,0},{20,4},{24,8},{28,12},{1,17},{... | collective-permute-start | bytes 589832 | tf_op jit(solution)/shard_map/ppermute | solution.py:227
  31.5 0.0 collective-permute-done.13.low_ref
  31.5 2.6 %collective-permute-start.7 = (bf16[2,32,768]{2,1,0:T(8,128)(2,1)S(1)}, bf16[2,32,768]{2,1,0:T(8,128)(2,1)S(1)}, u32[]{:S(2)}, u32[]{:S(2)}) collective-permute-start(bf16[2,32,768]{2,1,0:T(8,128)(2,1)S(1)} %get-tuple-element.35), channel_id=1, source_target_pairs={{0,2},{1,3},{2,0},{3,1},{4,6},{5,7},{6,4},{7,5},{8,10},{9,11},{10,... | collective-permute-start | bytes 294920 | tf_op jit(solution)/shard_map/ppermute | solution.py:311
  34.1 0.8 %shard_map.73 = (bf16[2,2,32,768]{3,2,1,0:T(8,128)(2,1)S(1)}, bf16[2,2,32,768]{3,2,1,0:T(8,128)(2,1)S(1)}) custom-call(bf16[2,32,1536]{2,1,0:T(8,128)(2,1)S(1)} %collective-permute-done.12.high_ref, bf16[2,32,1536]{2,1,0:T(8,128)(2,1)S(1)} %collective-permute-done.13.low_ref, bf16[2,1536,768]{2,1,0:T(8,128)(2,1)S(1)} %shard_map.66.refs_3_.turned_ref, ...), custom_call_target="tpu_custom_call" | custom-call | tf_op jit(solution)/shard_map/pallas_call | solution.py:294
  34.9 1.2 %collective-permute-start.14 = (bf16[2,2,32,768]{3,2,1,0:T(8,128)(2,1)S(1)}, bf16[2,2,32,768]{3,2,1,0:T(8,128)(2,1)S(1)}, u32[]{:S(2)}, u32[]{:S(2)}) collective-permute-start(bf16[2,2,32,768]{3,2,1,0:T(8,128)(2,1)S(1)} %get-tuple-element.41), channel_id=1, source_target_pairs={{0,1},{1,0},{2,3},{3,2},{4,5},{5,4},{6,7},{7,6},{8,9},{9,8},{10,11... | collective-permute-start | bytes 589832 | tf_op jit(solution)/shard_map/ppermute | solution.py:225
  36.1 0.0 collective-permute-done.10.came_ref
  36.2 1.8 %collective-permute-done.7.refs_2_.refs_0_ = bf16[2,32,768]{2,1,0:T(8,128)(2,1)S(1)} collective-permute-done((bf16[2,32,768]{2,1,0:T(8,128)(2,1)S(1)}, bf16[2,32,768]{2,1,0:T(8,128)(2,1)S(1)}, u32[]{:S(2)}, u32[]{:S(2)}) %collective-permute-start.7) | collective-permute-done | bytes 98336 | tf_op jit(solution)/shard_map/ppermute | solution.py:311
  38.0 0.8 %shard_map.76 = (bf16[2,2,32,768]{3,2,1,0:T(8,128)(2,1)S(1)}, bf16[2,2,32,768]{3,2,1,0:T(8,128)(2,1)S(1)}) custom-call(bf16[2,32,1536]{2,1,0:T(8,128)(2,1)S(1)} %collective-permute-done.18.high_ref, bf16[2,32,1536]{2,1,0:T(8,128)(2,1)S(1)} %collective-permute-done.19.low_ref, bf16[2,1536,768]{2,1,0:T(8,128)(2,1)S(1)} %shard_map.66.refs_3_.turned_ref, ...), custom_call_target="tpu_custom_call" | custom-call | tf_op jit(solution)/shard_map/pallas_call | solution.py:294
  38.8 1.0 %collective-permute-start.20 = (bf16[2,2,32,768]{3,2,1,0:T(8,128)(2,1)S(1)}, bf16[2,2,32,768]{3,2,1,0:T(8,128)(2,1)S(1)}, u32[]{:S(2)}, u32[]{:S(2)}) collective-permute-start(bf16[2,2,32,768]{3,2,1,0:T(8,128)(2,1)S(1)} %get-tuple-element.45), channel_id=1, source_target_pairs={{0,1},{1,0},{2,3},{3,2},{4,5},{5,4},{6,7},{7,6},{8,9},{9,8},{10,11... | collective-permute-start | bytes 589832 | tf_op jit(solution)/shard_map/ppermute | solution.py:225
  39.7 2.6 %collective-permute-start.11 = (bf16[2,32,768]{2,1,0:T(8,128)(2,1)S(1)}, bf16[2,32,768]{2,1,0:T(8,128)(2,1)S(1)}, u32[]{:S(2)}, u32[]{:S(2)}) collective-permute-start(bf16[2,32,768]{2,1,0:T(8,128)(2,1)S(1)} %get-tuple-element.39), channel_id=1, source_target_pairs={{0,10},{1,11},{2,16},{3,17},{4,14},{5,15},{6,20},{7,21},{8,2},{9,3... | collective-permute-start | bytes 294920 | tf_op jit(solution)/shard_map/ppermute | solution.py:311
  42.3 0.1 collective-permute-done.14.came_ref
  42.5 2.2 %collective-permute-start.16 = (bf16[2,32,768]{2,1,0:T(8,128)(2,1)S(1)}, bf16[2,32,768]{2,1,0:T(8,128)(2,1)S(1)}, u32[]{:S(2)}, u32[]{:S(2)}) collective-permute-start(bf16[2,32,768]{2,1,0:T(8,128)(2,1)S(1)} %get-tuple-element.43.order_ref), channel_id=1, source_target_pairs={{0,18},{1,19},{2,8},{3,9},{4,22},{5,23},{6,12},{7,13},{8,26},{9,27... | collective-permute-start | bytes 294920 | tf_op jit(solution)/shard_map/ppermute | solution.py:311
  44.7 0.9 %collective-permute-start.15 = (bf16[2,32,768]{2,1,0:T(8,128)(2,1)S(1)}, bf16[2,32,768]{2,1,0:T(8,128)(2,1)S(1)}, u32[]{:S(2)}, u32[]{:S(2)}) collective-permute-start(bf16[2,32,768]{2,1,0:T(8,128)(2,1)S(1)} %shard_map.75), channel_id=1, source_target_pairs={{0,16},{1,17},{2,10},{3,11},{4,20},{5,21},{6,14},{7,15},{8,24},{9,... | collective-permute-start | bytes 294920 | tf_op jit(solution)/shard_map/ppermute | solution.py:311
  45.7 1.2 %collective-permute-start.17 = (bf16[2,32,768]{2,1,0:T(8,128)(2,1)S(1)}, bf16[2,32,768]{2,1,0:T(8,128)(2,1)S(1)}, u32[]{:S(2)}, u32[]{:S(2)}) collective-permute-start(bf16[2,32,768]{2,1,0:T(8,128)(2,1)S(1)} %get-tuple-element.44), channel_id=1, source_target_pairs={{0,8},{1,9},{2,18},{3,19},{4,12},{5,13},{6,22},{7,23},{8,0},{9,1},... | collective-permute-start | bytes 294920 | tf_op jit(solution)/shard_map/ppermute | solution.py:311
  46.9 0.0 collective-permute-done.11.refs_0_.refs_2_
  46.9 0.0 collective-permute-done.20.came_ref
  47.0 4.3 %collective-permute-start.21 = (bf16[2,32,768]{2,1,0:T(8,128)(2,1)S(1)}, bf16[2,32,768]{2,1,0:T(8,128)(2,1)S(1)}, u32[]{:S(2)}, u32[]{:S(2)}) collective-permute-start(bf16[2,32,768]{2,1,0:T(8,128)(2,1)S(1)} %get-tuple-element.47), channel_id=1, source_target_pairs={{0,26},{1,27},{2,24},{3,25},{4,30},{5,31},{6,28},{7,29},{8,18},{9,... | collective-permute-start | bytes 294920 | tf_op jit(solution)/shard_map/ppermute | solution.py:311
  51.2 2.0 %collective-permute-start.22 = (bf16[2,32,768]{2,1,0:T(8,128)(2,1)S(1)}, bf16[2,32,768]{2,1,0:T(8,128)(2,1)S(1)}, u32[]{:S(2)}, u32[]{:S(2)}) collective-permute-start(bf16[2,32,768]{2,1,0:T(8,128)(2,1)S(1)} %get-tuple-element.48), channel_id=1, source_target_pairs={{0,24},{1,25},{2,26},{3,27},{4,28},{5,29},{6,30},{7,31},{8,16},{9,... | collective-permute-start | bytes 294920 | tf_op jit(solution)/shard_map/ppermute | solution.py:311
  53.2 1.1 %collective-permute-done.21.refs_6_ = bf16[2,32,768]{2,1,0:T(8,128)(2,1)S(1)} collective-permute-done((bf16[2,32,768]{2,1,0:T(8,128)(2,1)S(1)}, bf16[2,32,768]{2,1,0:T(8,128)(2,1)S(1)}, u32[]{:S(2)}, u32[]{:S(2)}) %collective-permute-start.21) | collective-permute-done | bytes 98336 | tf_op jit(solution)/shard_map/ppermute | solution.py:311
  54.3 2.4 %collective-permute-done.22.refs_7_ = bf16[2,32,768]{2,1,0:T(8,128)(2,1)S(1)} collective-permute-done((bf16[2,32,768]{2,1,0:T(8,128)(2,1)S(1)}, bf16[2,32,768]{2,1,0:T(8,128)(2,1)S(1)}, u32[]{:S(2)}, u32[]{:S(2)}) %collective-permute-start.22) | collective-permute-done | bytes 98336 | tf_op jit(solution)/shard_map/ppermute | solution.py:311
  56.7 0.8 %shard_map.78 = bf16[32,6144]{1,0:T(8,128)(2,1)} custom-call(bf16[2,32,768]{2,1,0:T(8,128)(2,1)S(1)} %collective-permute-done.7.refs_2_.refs_0_, bf16[2,32,768]{2,1,0:T(8,128)(2,1)S(1)} %get-tuple-element.36.refs_1_, bf16[2,32,768]{2,1,0:T(8,128)(2,1)S(1)} %collective-permute-done.11.refs_0_.refs_2_, ...), custom_call_target="tpu_custom_call" | custom-call | tf_op jit(solution)/shard_map/pallas_call | solution.py:338
  (13 shorter events, 0.2 us)
Async XLA Ops:
  0.0 12.2 %collective-permute-start.5 = (bf16[768,1536]{1,0:T(8,128)(2,1)}, bf16[768,1536]{1,0:T(8,128)(2,1)S(1)}, u32[]{:S(2)}, u32[]{:S(2)}) collective-permute-start(bf16[768,1536]{1,0:T(8,128)(2,1)} %mine_hbm.1), channel_id=1, source_target_pairs={{0,4},{4,0},{8,12},{12,8},{16,20},{20,16},{24,28},{28,24},{1,5},{5... | collective-permute-start | bytes 7077896 | tf_op jit(solution)/shard_map/ppermute | solution.py:227
  2.5 6.0 %collective-permute-start = (bf16[2,16,1536]{2,1,0:T(8,128)(2,1)S(1)}, bf16[2,16,1536]{2,1,0:T(8,128)(2,1)S(1)}, u32[]{:S(2)}, u32[]{:S(2)}) collective-permute-start(bf16[2,16,1536]{2,1,0:T(8,128)(2,1)S(1)} %get-tuple-element.31.refs_0_), channel_id=1, source_target_pairs={{0,8},{4,12},{8,0},{12,4},{16,24},{20,28},{24,16},{28,20},{1,9},{5... | collective-permute-start | bytes 294920 | tf_op jit(solution)/shard_map/ppermute | solution.py:227
  5.1 6.1 %collective-permute-start.1 = (bf16[2,16,1536]{2,1,0:T(8,128)(2,1)S(1)}, bf16[2,16,1536]{2,1,0:T(8,128)(2,1)S(1)}, u32[]{:S(2)}, u32[]{:S(2)}) collective-permute-start(bf16[2,16,1536]{2,1,0:T(8,128)(2,1)S(1)} %get-tuple-element.31.refs_0_), channel_id=1, source_target_pairs={{0,16},{4,20},{8,24},{12,28},{16,0},{20,4},{24,8},{28,12},{1,17},{... | collective-permute-start | bytes 294920 | tf_op jit(solution)/shard_map/ppermute | solution.py:227
  6.6 5.5 %collective-permute-start.2 = (bf16[2,16,1536]{2,1,0:T(8,128)(2,1)S(1)}, bf16[2,16,1536]{2,1,0:T(8,128)(2,1)S(1)}, u32[]{:S(2)}, u32[]{:S(2)}) collective-permute-start(bf16[2,16,1536]{2,1,0:T(8,128)(2,1)S(1)} %get-tuple-element.31.refs_0_), channel_id=1, source_target_pairs={{0,24},{4,28},{8,16},{12,20},{16,8},{20,12},{24,0},{28,4},{1,25},{... | collective-permute-start | bytes 294920 | tf_op jit(solution)/shard_map/ppermute | solution.py:227
  6.6 8.0 %collective-permute-start.4 = (bf16[2,64,1536]{2,1,0:T(8,128)(2,1)S(1)}, bf16[2,64,1536]{2,1,0:T(8,128)(2,1)S(1)}, u32[]{:S(2)}, u32[]{:S(2)}) collective-permute-start(bf16[2,64,1536]{2,1,0:T(8,128)(2,1)S(1)} %get-tuple-element.32), channel_id=1, source_target_pairs={{0,4},{4,8},{8,12},{12,16},{16,20},{20,24},{24,28},{1,5},{5,9},{9,... | collective-permute-start | bytes 1179656 | tf_op jit(solution)/shard_map/ppermute | solution.py:249
  12.2 2.5 %collective-permute-start.3 = (bf16[4,2,16,1536]{3,2,1,0:T(8,128)(2,1)S(1)}, bf16[4,2,16,1536]{3,2,1,0:T(8,128)(2,1)S(1)}, u32[]{:S(2)}, u32[]{:S(2)}) collective-permute-start(bf16[4,2,16,1536]{3,2,1,0:T(8,128)(2,1)S(1)} %shard_map.65.order_ref.refs_0_.refs_1_), channel_id=1, source_target_pairs={{0,4},{4,0},{8,12},{12,8},{16,20},{20,16},{24,28},{28,24},{1,5},{5... | collective-permute-start | bytes 1179656 | tf_op jit(solution)/shard_map/ppermute | solution.py:227
  15.3 9.2 %collective-permute-start.9 = (bf16[2,32,1536]{2,1,0:T(8,128)(2,1)S(1)}, bf16[2,32,1536]{2,1,0:T(8,128)(2,1)S(1)}, u32[]{:S(2)}, u32[]{:S(2)}) collective-permute-start(bf16[2,32,1536]{2,1,0:T(8,128)(2,1)S(1)} %bitcast.5), channel_id=1, source_target_pairs={{0,16},{4,20},{8,24},{12,28},{16,0},{20,4},{24,8},{28,12},{1,17},{... | collective-permute-start | bytes 589832 | tf_op jit(solution)/shard_map/ppermute | solution.py:227
  20.0 7.0 %collective-permute-start.8 = (bf16[2,32,1536]{2,1,0:T(8,128)(2,1)S(1)}, bf16[2,32,1536]{2,1,0:T(8,128)(2,1)S(1)}, u32[]{:S(2)}, u32[]{:S(2)}) collective-permute-start(bf16[2,32,1536]{2,1,0:T(8,128)(2,1)S(1)} %bitcast.2), channel_id=1, source_target_pairs={{0,8},{4,12},{8,0},{12,4},{16,24},{20,28},{24,16},{28,20},{1,9},{5... | collective-permute-start | bytes 589832 | tf_op jit(solution)/shard_map/ppermute | solution.py:227
  21.4 9.1 %collective-permute-start.6 = (bf16[2,2,32,768]{3,2,1,0:T(8,128)(2,1)S(1)}, bf16[2,2,32,768]{3,2,1,0:T(8,128)(2,1)S(1)}, u32[]{:S(2)}, u32[]{:S(2)}) collective-permute-start(bf16[2,2,32,768]{3,2,1,0:T(8,128)(2,1)S(1)} %get-tuple-element.33), channel_id=1, source_target_pairs={{0,1},{1,0},{2,3},{3,2},{4,5},{5,4},{6,7},{7,6},{8,9},{9,8},{10,11... | collective-permute-start | bytes 589832 | tf_op jit(solution)/shard_map/ppermute | solution.py:225
  23.1 8.4 %collective-permute-start.13 = (bf16[2,32,1536]{2,1,0:T(8,128)(2,1)S(1)}, bf16[2,32,1536]{2,1,0:T(8,128)(2,1)S(1)}, u32[]{:S(2)}, u32[]{:S(2)}) collective-permute-start(bf16[2,32,1536]{2,1,0:T(8,128)(2,1)S(1)} %bitcast.7), channel_id=1, source_target_pairs={{0,8},{4,12},{8,0},{12,4},{16,24},{20,28},{24,16},{28,20},{1,9},{5... | collective-permute-start | bytes 589832 | tf_op jit(solution)/shard_map/ppermute | solution.py:227
  24.5 9.6 %collective-permute-start.12 = (bf16[2,32,1536]{2,1,0:T(8,128)(2,1)S(1)}, bf16[2,32,1536]{2,1,0:T(8,128)(2,1)S(1)}, u32[]{:S(2)}, u32[]{:S(2)}) collective-permute-start(bf16[2,32,1536]{2,1,0:T(8,128)(2,1)S(1)} %bitcast.4), channel_id=1, source_target_pairs={{0,16},{4,20},{8,24},{12,28},{16,0},{20,4},{24,8},{28,12},{1,17},{... | collective-permute-start | bytes 589832 | tf_op jit(solution)/shard_map/ppermute | solution.py:227
  27.8 8.3 %collective-permute-start.10 = (bf16[2,2,32,768]{3,2,1,0:T(8,128)(2,1)S(1)}, bf16[2,2,32,768]{3,2,1,0:T(8,128)(2,1)S(1)}, u32[]{:S(2)}, u32[]{:S(2)}) collective-permute-start(bf16[2,2,32,768]{3,2,1,0:T(8,128)(2,1)S(1)} %get-tuple-element.37), channel_id=1, source_target_pairs={{0,1},{1,0},{2,3},{3,2},{4,5},{5,4},{6,7},{7,6},{8,9},{9,8},{10,11... | collective-permute-start | bytes 589832 | tf_op jit(solution)/shard_map/ppermute | solution.py:225
  29.7 8.2 %collective-permute-start.19 = (bf16[2,32,1536]{2,1,0:T(8,128)(2,1)S(1)}, bf16[2,32,1536]{2,1,0:T(8,128)(2,1)S(1)}, u32[]{:S(2)}, u32[]{:S(2)}) collective-permute-start(bf16[2,32,1536]{2,1,0:T(8,128)(2,1)S(1)} %collective-permute-done.9.low_ref), channel_id=1, source_target_pairs={{0,8},{4,12},{8,0},{12,4},{16,24},{20,28},{24,16},{28,20},{1,9},{5... | collective-permute-start | bytes 589832 | tf_op jit(solution)/shard_map/ppermute | solution.py:227
  30.5 7.4 %collective-permute-start.18 = (bf16[2,32,1536]{2,1,0:T(8,128)(2,1)S(1)}, bf16[2,32,1536]{2,1,0:T(8,128)(2,1)S(1)}, u32[]{:S(2)}, u32[]{:S(2)}) collective-permute-start(bf16[2,32,1536]{2,1,0:T(8,128)(2,1)S(1)} %collective-permute-done.8.high_ref), channel_id=1, source_target_pairs={{0,16},{4,20},{8,24},{12,28},{16,0},{20,4},{24,8},{28,12},{1,17},{... | collective-permute-start | bytes 589832 | tf_op jit(solution)/shard_map/ppermute | solution.py:227
  31.5 6.5 %collective-permute-start.7 = (bf16[2,32,768]{2,1,0:T(8,128)(2,1)S(1)}, bf16[2,32,768]{2,1,0:T(8,128)(2,1)S(1)}, u32[]{:S(2)}, u32[]{:S(2)}) collective-permute-start(bf16[2,32,768]{2,1,0:T(8,128)(2,1)S(1)} %get-tuple-element.35), channel_id=1, source_target_pairs={{0,2},{1,3},{2,0},{3,1},{4,6},{5,7},{6,4},{7,5},{8,10},{9,11},{10,... | collective-permute-start | bytes 294920 | tf_op jit(solution)/shard_map/ppermute | solution.py:311
  34.9 7.5 %collective-permute-start.14 = (bf16[2,2,32,768]{3,2,1,0:T(8,128)(2,1)S(1)}, bf16[2,2,32,768]{3,2,1,0:T(8,128)(2,1)S(1)}, u32[]{:S(2)}, u32[]{:S(2)}) collective-permute-start(bf16[2,2,32,768]{3,2,1,0:T(8,128)(2,1)S(1)} %get-tuple-element.41), channel_id=1, source_target_pairs={{0,1},{1,0},{2,3},{3,2},{4,5},{5,4},{6,7},{7,6},{8,9},{9,8},{10,11... | collective-permute-start | bytes 589832 | tf_op jit(solution)/shard_map/ppermute | solution.py:225
  38.8 8.1 %collective-permute-start.20 = (bf16[2,2,32,768]{3,2,1,0:T(8,128)(2,1)S(1)}, bf16[2,2,32,768]{3,2,1,0:T(8,128)(2,1)S(1)}, u32[]{:S(2)}, u32[]{:S(2)}) collective-permute-start(bf16[2,2,32,768]{3,2,1,0:T(8,128)(2,1)S(1)} %get-tuple-element.45), channel_id=1, source_target_pairs={{0,1},{1,0},{2,3},{3,2},{4,5},{5,4},{6,7},{7,6},{8,9},{9,8},{10,11... | collective-permute-start | bytes 589832 | tf_op jit(solution)/shard_map/ppermute | solution.py:225
  39.7 7.2 %collective-permute-start.11 = (bf16[2,32,768]{2,1,0:T(8,128)(2,1)S(1)}, bf16[2,32,768]{2,1,0:T(8,128)(2,1)S(1)}, u32[]{:S(2)}, u32[]{:S(2)}) collective-permute-start(bf16[2,32,768]{2,1,0:T(8,128)(2,1)S(1)} %get-tuple-element.39), channel_id=1, source_target_pairs={{0,10},{1,11},{2,16},{3,17},{4,14},{5,15},{6,20},{7,21},{8,2},{9,3... | collective-permute-start | bytes 294920 | tf_op jit(solution)/shard_map/ppermute | solution.py:311
  42.5 10.7 %collective-permute-start.16 = (bf16[2,32,768]{2,1,0:T(8,128)(2,1)S(1)}, bf16[2,32,768]{2,1,0:T(8,128)(2,1)S(1)}, u32[]{:S(2)}, u32[]{:S(2)}) collective-permute-start(bf16[2,32,768]{2,1,0:T(8,128)(2,1)S(1)} %get-tuple-element.43.order_ref), channel_id=1, source_target_pairs={{0,18},{1,19},{2,8},{3,9},{4,22},{5,23},{6,12},{7,13},{8,26},{9,27... | collective-permute-start | bytes 294920 | tf_op jit(solution)/shard_map/ppermute | solution.py:311
  44.7 8.5 %collective-permute-start.15 = (bf16[2,32,768]{2,1,0:T(8,128)(2,1)S(1)}, bf16[2,32,768]{2,1,0:T(8,128)(2,1)S(1)}, u32[]{:S(2)}, u32[]{:S(2)}) collective-permute-start(bf16[2,32,768]{2,1,0:T(8,128)(2,1)S(1)} %shard_map.75), channel_id=1, source_target_pairs={{0,16},{1,17},{2,10},{3,11},{4,20},{5,21},{6,14},{7,15},{8,24},{9,... | collective-permute-start | bytes 294920 | tf_op jit(solution)/shard_map/ppermute | solution.py:311
  45.7 7.6 %collective-permute-start.17 = (bf16[2,32,768]{2,1,0:T(8,128)(2,1)S(1)}, bf16[2,32,768]{2,1,0:T(8,128)(2,1)S(1)}, u32[]{:S(2)}, u32[]{:S(2)}) collective-permute-start(bf16[2,32,768]{2,1,0:T(8,128)(2,1)S(1)} %get-tuple-element.44), channel_id=1, source_target_pairs={{0,8},{1,9},{2,18},{3,19},{4,12},{5,13},{6,22},{7,23},{8,0},{9,1},... | collective-permute-start | bytes 294920 | tf_op jit(solution)/shard_map/ppermute | solution.py:311
  47.0 7.4 %collective-permute-start.21 = (bf16[2,32,768]{2,1,0:T(8,128)(2,1)S(1)}, bf16[2,32,768]{2,1,0:T(8,128)(2,1)S(1)}, u32[]{:S(2)}, u32[]{:S(2)}) collective-permute-start(bf16[2,32,768]{2,1,0:T(8,128)(2,1)S(1)} %get-tuple-element.47), channel_id=1, source_target_pairs={{0,26},{1,27},{2,24},{3,25},{4,30},{5,31},{6,28},{7,29},{8,18},{9,... | collective-permute-start | bytes 294920 | tf_op jit(solution)/shard_map/ppermute | solution.py:311
  51.2 5.5 %collective-permute-start.22 = (bf16[2,32,768]{2,1,0:T(8,128)(2,1)S(1)}, bf16[2,32,768]{2,1,0:T(8,128)(2,1)S(1)}, u32[]{:S(2)}, u32[]{:S(2)}) collective-permute-start(bf16[2,32,768]{2,1,0:T(8,128)(2,1)S(1)} %get-tuple-element.48), channel_id=1, source_target_pairs={{0,24},{1,25},{2,26},{3,27},{4,28},{5,29},{6,30},{7,31},{8,16},{9,... | collective-permute-start | bytes 294920 | tf_op jit(solution)/shard_map/ppermute | solution.py:311
